TPU v7x, 32 devices: a whole 2x2x4 slice. The times are simulated.
32 devices in a mesh: hst: 8 (over z, x), doc: 4 (over y, core).
Axes of the slice: x: 2, y: 2, z: 4, core: 2. Of those that a mesh axis runs over, the one named last changes fastest.
Arguments:
- docs: bfloat16 [262144, 768], P(('hst', 'doc')), may hold values from -400 to 400, as said below
- w_in: bfloat16 [768, 256], replicated, may hold values from -0.21875 to 0.21875
- w_out: bfloat16 [256, 64], replicated, may hold values from -0.375 to 0.375
- doc_host: int32 [262144], P(('hst', 'doc')), may hold values from 0 to 2047
- tiles: bfloat16 [2048, 128, 128], P(('hst', 'doc')), may hold values from 0 to 10, as said below
- dst_block: int32 [2048], P(('hst', 'doc')), may hold values from 0 to 15
- src_block: int32 [2048], P(('hst', 'doc')), may hold values from 0 to 127
- tile_count: int32 [32], P(('hst', 'doc')), may hold values from 1 to 64, as said below
- teleport: int32 [16384], P('hst'), may hold values 0 or 1
Outputs:
- scores: float32 [16384, 64], P(('hst', 'doc'))
Inputs may be any that keep to these rules, and one draw needn't show every extreme that they name: `docs`: embeddings stay in the stated range. `tiles`: link weights are nonnegative. `tile_count`: some device uses all 64 slots.
All inputs are finite; a program needn't handle non-finite values. No bound on the sum of `teleport` on one device may be relied on, other than what follows from the above.
Results may differ from a plain program's by a relative error of at most 0.00066.
Values may be sent and summed in bfloat16 or wider, within the bound.
No kernel may reach another device: no remote copies, remote signals or barrier semaphores. Data moves between devices by JAX's collectives and lax.ppermute only.
A program may use at most 128 MiB of HBM per device.

v0:
```python
import jax
import jax.numpy as jnp
from jax import lax
from jax.sharding import PartitionSpec as P

HOPS = 3


def body(docs, w_in, w_out, doc_host, tiles, dst_block, src_block, tile_count, teleport):
    host_dev = teleport.shape[0]
    block = tiles.shape[1]
    topics = w_out.shape[1]
    slots = tiles.shape[0]
    hosts_all = host_dev * lax.axis_size("hst")
    nblocks = hosts_all // block
    hidden = jax.nn.gelu(
        jnp.dot(docs, w_in, preferred_element_type=jnp.float32), approximate=True
    ).astype(jnp.bfloat16)
    probs = jax.nn.softmax(jnp.dot(hidden, w_out, preferred_element_type=jnp.float32), axis=-1)
    local_topic = jax.ops.segment_sum(probs, doc_host, num_segments=host_dev)
    used = (jnp.arange(slots) < tile_count[0]).astype(jnp.float32)
    colsum = jnp.sum(tiles, axis=1, dtype=jnp.float32)
    src_onehot = (src_block[:, None] == jnp.arange(nblocks)[None, :]).astype(jnp.float32) * used[
        :, None
    ]
    degree_blocks = jnp.dot(src_onehot.T, colsum, precision=lax.Precision.HIGHEST)
    degree = lax.psum(degree_blocks, ("hst", "doc")).reshape(hosts_all)
    own_degree = lax.dynamic_slice_in_dim(degree, lax.axis_index("hst") * host_dev, host_dev)
    inverse = 1.0 / jnp.maximum(own_degree, 1.0)
    dst_onehot = (dst_block[:, None] == jnp.arange(host_dev // block)[None, :]).astype(
        jnp.float32
    ) * used[:, None]
    member = teleport.astype(jnp.float32)
    rows = host_dev // lax.axis_size("doc")
    host_topic = lax.psum(local_topic, "doc")
    mass = lax.psum(jnp.sum(member[:, None] * host_topic, axis=0), "hst")
    tele = member[:, None] * host_topic / mass
    state = tele
    for hop in range(HOPS):
        sent = (state * inverse[:, None]).astype(jnp.bfloat16)
        full = lax.all_gather(sent, "hst", axis=0, tiled=True)
        slabs = full.reshape(nblocks, block, topics)[src_block]
        prod = jnp.einsum("kij,kjt->kit", tiles, slabs, preferred_element_type=jnp.float32)
        gathered = jnp.einsum("kb,kit->bit", dst_onehot, prod, precision=lax.Precision.HIGHEST)
        inflow = lax.psum(gathered.reshape(host_dev, topics), "doc")
        state = 0.85 * inflow + 0.15 * tele
    result = lax.dynamic_slice_in_dim(state, lax.axis_index("doc") * rows, rows)
    return hosts_all * result


def solution(mesh):
    placed = (
        P(("hst", "doc"), None),
        P(),
        P(),
        P(("hst", "doc")),
        P(("hst", "doc"), None, None),
        P(("hst", "doc")),
        P(("hst", "doc")),
        P(("hst", "doc")),
        P("hst"),
    )
    return jax.shard_map(
        body, mesh=mesh, in_specs=placed, out_specs=P(("hst", "doc"), None), check_vma=False
    )
```

profile of v0, /device:TPU:0, one launch (start us, length us, event | category | flops | bytes accessed | tf_op | source)
XLA Modules:
  0.0 479.3 jit_solution(9004848619201945616)
XLA Ops:
  7.3 2.1 convert_reduce_fusion
  9.4 1.0 convolution_bitcast_fusion
  10.4 0.0 all-reduce.8.cloned.1.call-update
  10.4 0.0 all-reduce.6.cloned.1.call-start
  10.5 0.0 copy-done
  10.5 0.0 copy-done.13
  10.5 8.6 %fusion.48 = (f32[8192]{0:T(1024)S(1)}, f32[8192,64]{0,1:T(8,128)S(1)}) fusion(bf16[256,64]{0,1:T(8,128)(2,1)S(1)} %copy-done.13, bf16[8192,768]{1,0:T(8,128)(2,1)} %param.9, bf16[768,256]{1,0:T(8,128)(2,1)S(1)} %copy-done), kind=kOutput, calls=%fused_computation.78 | convolution fusion | flops 3509051392 | bytes 15138816 | tf_op jit(solution)/shard_map/dot_general | solution.py:19
  19.1 1.3 copy-done.2
  20.5 0.3 fusion.17
  20.8 1.9 fusion.16
  22.7 2.7 copy.18
  25.5 44.5 %scatter_custom_fusion = f32[2048,64]{1,0:T(8,128)S(1)} fusion(s32[8192]{0:T(1024)} %param.12, f32[8192,64]{1,0:T(8,128)} %copy.18, f32[]{:T(128)} %constant.17.clone.1), kind=kCustom, calls=%fused_computation.37 | custom fusion | flops 524288 | bytes 524800 | tf_op jit(solution)/shard_map/scatter-add | solution.py:20
  70.0 1.1 copy.19
  71.1 0.0 all-reduce.6.cloned.1.call-update
  71.2 0.0 all-gather.4.cloned.1.call-start
  71.2 62.0 %all-reduce.8.cloned.1.call-done = f32[16384]{0:T(1024)} async-done(((f32[16384]{0:T(1024)}), f32[16384]{0:T(1024)}) %all-reduce.8.cloned.1.call-update) | async-done | bytes 65552 | tf_op jit(solution)/shard_map/psum | solution.py:27
  133.2 0.7 maximum_divide_fusion
  133.9 35.7 %all-reduce.6.cloned.1.call-done = f32[2048,64]{0,1:T(8,128)} async-done(((f32[2048,64]{0,1:T(8,128)}), f32[2048,64]{0,1:T(8,128)}) %all-reduce.6.cloned.1.call-update) | async-done | bytes 524304 | tf_op jit(solution)/shard_map/psum | solution.py:35
  169.6 1.2 multiply_reduce_fusion
  170.8 21.4 %psum.43 = f32[64]{0:T(128)S(1)} all-reduce(f32[64]{0:T(128)S(1)} %multiply_reduce_fusion), channel_id=1, replica_groups=mesh['hst'=8,'doc'=4] {'hst'}, use_global_device_ids=true, to_apply=%region_5.0 | all-reduce | flops 64 | bytes 512 | tf_op jit(solution)/shard_map/psum | solution.py:36
  192.2 1.9 multiply_convert_fusion.2
  194.0 0.0 all-gather.4.cloned.1.call-update
  194.0 0.0 all-reduce.10.cloned.1.call-start
  194.1 0.6 pad_clamp_fusion
  194.7 45.0 %all-gather.4.cloned.1.call-done = bf16[16384,64]{0,1:T(8,128)(2,1)} async-done(((bf16[2048,64]{0,1:T(8,128)(2,1)}), bf16[16384,64]{0,1:T(8,128)(2,1)}) %all-gather.4.cloned.1.call-update) | async-done | bytes 2097168 | tf_op jit(solution)/shard_map/all_gather | solution.py:41
  239.7 3.5 copy_bitcast_fusion.2
  243.2 2.6 gather_fusion
  245.9 0.0 copy-start.6
  245.9 1.5 convolution_bitcast_fusion.3
  247.4 0.0 copy-done.6
  247.4 0.0 copy-done.9
  247.4 0.0 copy-start.3
  247.4 0.0 copy-start.12
  247.5 2.2 fusion.14
  249.7 1.0 copy.46
  250.6 0.0 all-reduce.10.cloned.1.call-update
  250.7 0.0 all-gather.6.cloned.1.call-start
  250.7 31.8 %all-reduce.10.cloned.1.call-done = f32[2048,64]{0,1:T(8,128)} async-done(((f32[2048,64]{0,1:T(8,128)}), f32[2048,64]{0,1:T(8,128)}) %all-reduce.10.cloned.1.call-update) | async-done | bytes 524304 | tf_op jit(solution)/shard_map/psum | solution.py:45
  282.5 2.1 multiply_convert_fusion.1
  284.7 0.0 all-gather.6.cloned.1.call-update
  284.7 0.2 all-reduce.12.cloned.1.call-start
  284.9 49.2 %all-gather.6.cloned.1.call-done = bf16[16384,64]{0,1:T(8,128)(2,1)} async-done(((bf16[2048,64]{0,1:T(8,128)(2,1)}), bf16[16384,64]{0,1:T(8,128)(2,1)}) %all-gather.6.cloned.1.call-update) | async-done | bytes 2097168 | tf_op jit(solution)/shard_map/all_gather | solution.py:41
  334.1 3.5 copy_bitcast_fusion.1
  337.6 2.5 gather_fusion.1
  340.1 0.0 copy-start.7
  340.1 1.5 convolution_bitcast_fusion.2
  341.6 0.0 copy-done.10
  341.6 2.2 fusion.12
  343.9 1.0 copy.45
  344.8 0.0 all-reduce.12.cloned.1.call-update
  344.9 0.0 all-gather.8.cloned.1.call-start
  344.9 31.8 %all-reduce.12.cloned.1.call-done = f32[2048,64]{0,1:T(8,128)} async-done(((f32[2048,64]{0,1:T(8,128)}), f32[2048,64]{0,1:T(8,128)}) %all-reduce.12.cloned.1.call-update) | async-done | bytes 524304 | tf_op jit(solution)/shard_map/psum | solution.py:45
  376.7 1.8 multiply_convert_fusion
  378.5 0.0 all-gather.8.cloned.1.call-update
  378.6 0.0 all-reduce.14.cloned.1.call-start
  378.6 49.6 %all-gather.8.cloned.1.call-done = bf16[16384,64]{0,1:T(8,128)(2,1)} async-done(((bf16[2048,64]{0,1:T(8,128)(2,1)}), bf16[16384,64]{0,1:T(8,128)(2,1)}) %all-gather.8.cloned.1.call-update) | async-done | bytes 2097168 | tf_op jit(solution)/shard_map/all_gather | solution.py:41
  428.2 3.5 copy_bitcast_fusion
  431.7 2.5 gather_fusion.2
  434.2 1.5 convolution_bitcast_fusion.1
  435.7 2.2 fusion.10
  437.9 1.0 copy.44
  438.9 0.0 all-reduce.14.cloned.1.call-update
  438.9 31.9 %all-reduce.14.cloned.1.call-done = f32[2048,64]{0,1:T(8,128)} async-done(((f32[2048,64]{0,1:T(8,128)}), f32[2048,64]{0,1:T(8,128)}) %all-reduce.14.cloned.1.call-update) | async-done | bytes 524304 | tf_op jit(solution)/shard_map/psum | solution.py:45
  470.8 1.6 fusion.20
  (24 shorter events, 0.1 us)
Async XLA Ops:
  6.5 3.9 copy-start
  6.5 2.9 copy-start.14
  6.5 3.9 copy-start.13
  6.5 126.7 %all-reduce.8.cloned.1.call-start = ((), (), s32[]{:S(2)}) async-start(), calls=%async_computation.1 | async-start | bytes 131072 | tf_op jit(solution)/shard_map/psum | solution.py:27
  7.3 2.1 copy-start.8
  10.4 159.2 %all-reduce.6.cloned.1.call-start = ((), (), s32[]{:S(2)}) async-start(), calls=%async_computation | async-start | bytes 1048576 | tf_op jit(solution)/shard_map/psum | solution.py:35
  19.1 1.3 copy-start.2
  25.5 45.8 %copy-start.5 = (s32[2048]{0:T(1024)S(1)}, s32[2048]{0:T(1024)}, u32[]{:S(2)}) copy-start(s32[2048]{0:T(1024)} %param.17) | copy-start | bytes 24580
  71.2 168.6 %all-gather.4.cloned.1.call-start = ((), (), s32[]{:S(2)}) async-start(), calls=%async_computation.2 | async-start | bytes 2359296 | tf_op jit(solution)/shard_map/all_gather | solution.py:41
  192.2 47.6 %copy-start.11 = (f32[64]{0:T(128)}, f32[64]{0:T(128)S(1)}, u32[]{:S(2)}) copy-start(f32[64]{0:T(128)S(1)} %psum.43) | copy-start | bytes 772
  194.0 88.5 %all-reduce.10.cloned.1.call-start = ((), (), s32[]{:S(2)}) async-start(), calls=%async_computation.3 | async-start | bytes 1048576 | tf_op jit(solution)/shard_map/psum | solution.py:45
  243.2 2.6 copy-start.1
  245.9 1.6 copy-start.6
  245.9 1.5 copy-start.9
  247.4 35.1 %copy-start.3 = (f32[2048,64]{0,1:T(8,128)S(1)}, f32[2048,64]{0,1:T(8,128)}, u32[]{:S(2)}) copy-start(f32[2048,64]{0,1:T(8,128)} %all-reduce.6.cloned.1.call-done) | copy-start | bytes 1572868
  247.4 35.1 %copy-start.12 = (f32[64]{0:T(128)S(1)}, f32[64]{0:T(128)}, u32[]{:S(2)}) copy-start(f32[64]{0:T(128)} %copy-done.11) | copy-start | bytes 772
  250.7 83.4 %all-gather.6.cloned.1.call-start = ((), (), s32[]{:S(2)}) async-start(), calls=%async_computation.4 | async-start | bytes 2359296 | tf_op jit(solution)/shard_map/all_gather | solution.py:41
  284.7 92.0 %all-reduce.12.cloned.1.call-start = ((), (), s32[]{:S(2)}) async-start(), calls=%async_computation.5 | async-start | bytes 1048576 | tf_op jit(solution)/shard_map/psum | solution.py:45
  340.1 1.5 copy-start.7
  340.1 1.6 copy-start.10
  341.6 35.1 %copy-start.4 = (f32[2048,64]{0,1:T(8,128)S(1)}, f32[2048,64]{0,1:T(8,128)}, u32[]{:S(2)}) copy-start(f32[2048,64]{0,1:T(8,128)} %get-tuple-element.6) | copy-start | bytes 1572868
  344.9 83.3 %all-gather.8.cloned.1.call-start = ((), (), s32[]{:S(2)}) async-start(), calls=%async_computation.6 | async-start | bytes 2359296 | tf_op jit(solution)/shard_map/all_gather | solution.py:41
  378.6 92.2 %all-reduce.14.cloned.1.call-start = ((), (), s32[]{:S(2)}) async-start(), calls=%async_computation.7 | async-start | bytes 1048576 | tf_op jit(solution)/shard_map/psum | solution.py:45
Sparse Core Ops, SparseCore 0:
  12.9 120.2 all-reduce.7
  135.6 33.9 all-reduce.5
  194.2 45.5 all-gather.3
  250.8 31.6 all-reduce.9
  284.8 49.2 all-gather.5
  345.0 31.6 all-reduce.11
  378.9 49.2 all-gather.7
  439.1 31.6 all-reduce.13
where the time goes:
time: 480 us; the launch traced here: 479 us
  waiting for transfers between devices  337 us (70%)
  other arithmetic  58.8 us (12%)
  local copies, waits for them, and re-layouts  26.2 us (5%)
  blocking collectives  21.4 us (4%)
  matrix products  20.9 us (4%)
  between operations  14.5 us (3%)
    all_gather x3, waiting for transfers between devices, body(): full = lax.all_gather(sent, 'hst', axis=0, tiled=True)  144 us
    psum x3, waiting for transfers between devices, body(): inflow = lax.psum(gathered.reshape(host_dev, topics), 'doc')  95.5 us
    psum x1, waiting for transfers between devices, body(): degree = lax.psum(degree_blocks, ('hst', 'doc')).reshape(hosts_all)  62 us
    scatter-add x1, other arithmetic, body(): local_topic = jax.ops.segment_sum(probs, doc_host, num_segments=host_dev)  44.5 us
    psum x1, waiting for transfers between devices, body(): host_topic = lax.psum(local_topic, 'doc')  35.7 us
    psum x1, blocking collectives, body(): mass = lax.psum(jnp.sum(member[:, None] * host_topic, axis=0), 'hst')  21.4 us
    reshape x3, local copies, waits for them, and re-layouts, body(): slabs = full.reshape(nblocks, block, topics)[src_block]  10.5 us
  transfers between devices with their start and end apart: 8, of which 8 were waited for; matrix products, arithmetic and copies ran while one was open for 13% of the time, Pallas kernels for 0%

commit v1 on v0

v1 whole, which is shorter than its diff:
```python
import functools

import jax
import jax.numpy as jnp
from jax import lax
from jax.experimental import pallas as pl
from jax.experimental.pallas import tpu as pltpu
from jax.sharding import PartitionSpec as P

HOPS = 3
DIGITS = 4
DOC_BLOCK = 1024
GROUP = 8
LIFT = 2.0**64
NT = (((1,), (1,)), ((), ()))
MIB = 1 << 20


def xor_send(value, axis, step):
    size = lax.axis_size(axis)
    return lax.ppermute(value, axis, [(i, i ^ step) for i in range(size)])


def column_sum_kernel(meta, tiles, *rest):
    outs, total = rest[:-1], rest[-1]
    step = pl.program_id(0)

    @pl.when(step == 0)
    def _():
        total[...] = jnp.zeros_like(total)

    for i in range(GROUP):
        row = meta[step * GROUP + i]
        part = jnp.sum(tiles[i].astype(jnp.float32), axis=0, keepdims=True)
        total[pl.ds(row, 1), :] += part

    @pl.when(step == pl.num_programs(0) - 1)
    def _():
        rows = outs[0].shape[0]
        for j, out in enumerate(outs):
            out[...] = total[j * rows : (j + 1) * rows, :]


def column_sums(meta, tiles, parts, rows):
    slots, block, _ = tiles.shape
    shape = jax.ShapeDtypeStruct((rows, block), jnp.float32)
    return pl.pallas_call(
        column_sum_kernel,
        grid_spec=pltpu.PrefetchScalarGridSpec(
            num_scalar_prefetch=1,
            grid=(slots // GROUP,),
            in_specs=[pl.BlockSpec((GROUP, block, block), lambda i, m: (i, 0, 0))],
            out_specs=[pl.BlockSpec((rows, block), lambda i, m: (0, 0))] * parts,
            scratch_shapes=[pltpu.VMEM((parts * rows + 8, block), jnp.float32)],
        ),
        out_shape=[shape] * parts,
        compiler_params=pltpu.CompilerParams(vmem_limit_bytes=16 * MIB),
        cost_estimate=pl.CostEstimate(
            flops=tiles.size, bytes_accessed=tiles.size * 2, transcendentals=0
        ),
        name="column_sums",
    )(meta, tiles)


def documents_kernel(place, docs, w_in, w_out, host, *rest):
    outs, w_out_t, total = rest[:-2], rest[-2], rest[-1]
    step = pl.program_id(0)
    topics = w_out.shape[1]
    width = total.shape[1]

    @pl.when(step == 0)
    def _():
        total[...] = jnp.zeros_like(total)
        w_out_t[...] = w_out[...].astype(jnp.float32).T.astype(jnp.bfloat16)

    hidden = jax.nn.gelu(
        jnp.dot(docs[...], w_in[...], preferred_element_type=jnp.float32), approximate=True
    ).astype(jnp.bfloat16)
    logits = lax.dot_general(w_out_t[...], hidden, NT, preferred_element_type=jnp.float32)
    powers = jnp.exp(logits - jnp.max(logits, axis=0, keepdims=True))
    probs = powers * (1.0 / jnp.sum(powers, axis=0, keepdims=True))
    high = probs.astype(jnp.bfloat16)
    low = (probs - high.astype(jnp.float32)).astype(jnp.bfloat16)
    index = host[0]
    digit = index // width
    within = index - digit * width
    picks = [jnp.where(digit == j, 1.0, 0.0).astype(jnp.bfloat16) for j in range(DIGITS)]
    left = jnp.concatenate([high * p for p in picks] + [low * p for p in picks], axis=0)
    places = lax.broadcasted_iota(jnp.int32, (width, index.shape[1]), 0)
    right = jnp.where(places == within, 1.0, 0.0).astype(jnp.bfloat16)
    total[...] += lax.dot_general(left, right, NT, preferred_element_type=jnp.float32)

    @pl.when(step == pl.num_programs(0) - 1)
    def _():
        per = outs[0].shape[0]
        for j, out in enumerate(outs):
            first = (place[0] ^ j) * per
            for d in range(DIGITS):
                high_rows = pl.ds(pl.multiple_of(d * topics + first, 8), per)
                low_rows = pl.ds(pl.multiple_of((DIGITS + d) * topics + first, 8), per)
                out[:, d * width : (d + 1) * width] = total[high_rows, :] + total[low_rows, :]


def document_topics(place, docs, w_in, w_out, doc_host, hosts, split):
    count, depth = docs.shape
    hid, topics = w_out.shape
    per = topics // split
    width = hosts // DIGITS
    steps = count // DOC_BLOCK
    shape = jax.ShapeDtypeStruct((per, hosts), jnp.float32)
    return pl.pallas_call(
        documents_kernel,
        grid_spec=pltpu.PrefetchScalarGridSpec(
            num_scalar_prefetch=1,
            grid=(steps,),
            in_specs=[
                pl.BlockSpec((DOC_BLOCK, depth), lambda i, m: (i, 0)),
                pl.BlockSpec((depth, hid), lambda i, m: (0, 0)),
                pl.BlockSpec((hid, topics), lambda i, m: (0, 0)),
                pl.BlockSpec((1, 1, DOC_BLOCK), lambda i, m: (i, 0, 0)),
            ],
            out_specs=[pl.BlockSpec((per, hosts), lambda i, m: (0, 0))] * split,
            scratch_shapes=[
                pltpu.VMEM((topics, hid), jnp.bfloat16),
                pltpu.VMEM((2 * DIGITS * topics, width), jnp.float32),
            ],
        ),
        out_shape=[shape] * split,
        compiler_params=pltpu.CompilerParams(vmem_limit_bytes=40 * MIB),
        cost_estimate=pl.CostEstimate(
            flops=2 * count * (depth * hid + hid * topics + 2 * topics * hosts),
            bytes_accessed=docs.size * 2,
            transcendentals=count * (hid + topics),
        ),
        name="document_topics",
    )(place, docs, w_in, w_out, doc_host.reshape(steps, 1, DOC_BLOCK))


def start_kernel(split, teleport, *rest):
    sums, degrees = rest[:split], rest[split : 2 * split]
    sent, start, inverse = rest[2 * split :]
    block = inverse.shape[1]
    degree = sum(ref[...] for ref in degrees[1:]) + degrees[0][...]
    inv = 1.0 / jnp.maximum(degree, 1.0)
    inverse[...] = inv
    member = teleport[...].astype(jnp.float32) * LIFT
    mass = jnp.zeros((start.shape[0], 1), jnp.float32)
    for b in range(inv.shape[0]):
        cols = slice(b * block, (b + 1) * block)
        value = sum(ref[:, cols] for ref in sums[1:]) + sums[0][:, cols]
        value = value * member[b : b + 1, :]
        start[:, cols] = value
        sent[:, cols] = (value * inv[b : b + 1, :]).astype(jnp.bfloat16)
        mass = mass + jnp.sum(value, axis=1, keepdims=True)
    lane = lax.broadcasted_iota(jnp.int32, (start.shape[0], block), 1)
    first = mass.astype(jnp.bfloat16).astype(jnp.float32)
    second = (mass - first).astype(jnp.bfloat16).astype(jnp.float32)
    third = mass - first - second
    pieces = jnp.where(lane == 0, first, jnp.where(lane == 1, second, jnp.where(lane == 2, third, 0.0)))
    sent[:, inv.shape[0] * block :] = pieces.astype(jnp.bfloat16)


def start_values(teleport, sums, degrees):
    per, hosts = sums[0].shape
    blocks, block = degrees[0].shape
    return pl.pallas_call(
        functools.partial(start_kernel, len(sums)),
        out_shape=[
            jax.ShapeDtypeStruct((per, hosts + block), jnp.bfloat16),
            jax.ShapeDtypeStruct((per, hosts), jnp.float32),
            jax.ShapeDtypeStruct((blocks, block), jnp.float32),
        ],
        compiler_params=pltpu.CompilerParams(vmem_limit_bytes=16 * MIB),
        name="start_values",
    )(teleport.reshape(blocks, block), *sums, *degrees)


def hop_kernel(first, last, parts, split, meta, place, *rest):
    shards, tiles = rest[:parts], rest[parts : parts + split]
    tele, inverse = rest[parts + split : parts + split + 2]
    outs, slabs, inflow = rest[parts + split + 2 : -2], rest[-2], rest[-1]
    blocks, block = inverse.shape
    slots = tiles[0].shape[0] * pl.num_programs(0)
    span = meta.shape[0] // split
    step = pl.program_id(0)

    @pl.when(step == 0)
    def _():
        inflow[...] = jnp.zeros_like(inflow)
        slabs[parts * blocks] = jnp.zeros(slabs.shape[1:], slabs.dtype)
        for j, shard in enumerate(shards):
            for b in range(blocks):
                slabs[j * blocks + b] = shard[:, b * block : (b + 1) * block]

    for q in range(split):
        base = q * span

        @pl.when(step * GROUP < meta[base + 2 * slots])
        def _():
            products = []
            for i in range(GROUP):
                slab = slabs[meta[base + step * GROUP + i]]
                products.append(
                    lax.dot_general(slab, tiles[q][i], NT, preferred_element_type=jnp.float32)
                )
            for i in range(GROUP):
                inflow[meta[base + slots + step * GROUP + i]] += products[i]

    @pl.when(step == pl.num_programs(0) - 1)
    def _():
        if first:
            mass = sum(jnp.sum(s[:, blocks * block :].astype(jnp.float32), axis=1, keepdims=True) for s in shards)
        for b in range(blocks):
            cols = slice(b * block, (b + 1) * block)
            own = tele[:, cols]
            state = 0.85 * inflow[b] + 0.15 * own
            if first:
                state = state / mass
                outs[1][:, cols] = own / mass
            if last:
                inflow[b] = state
            else:
                outs[0][:, cols] = (state * inverse[b : b + 1, :]).astype(jnp.bfloat16)
        if last:
            count = outs[0].shape[1] // block
            for j, out in enumerate(outs):
                begin = (place[0] ^ j) * count
                for i in range(count):
                    out[:, i * block : (i + 1) * block] = inflow[begin + i]


def hop(first, last, meta, place, shards, tiles, tele, inverse):
    per, hosts = tele.shape
    blocks, block = inverse.shape
    parts, split = len(shards), len(tiles)
    slots = tiles[0].shape[0]
    whole = lambda i, m, p: (0, 0)
    if last:
        out_shape = [jax.ShapeDtypeStruct((per, hosts // split), jnp.float32)] * split
    else:
        out_shape = [jax.ShapeDtypeStruct((per, hosts), jnp.bfloat16)]
        if first:
            out_shape.append(jax.ShapeDtypeStruct((per, hosts), jnp.float32))
    return pl.pallas_call(
        functools.partial(hop_kernel, first, last, parts, split),
        grid_spec=pltpu.PrefetchScalarGridSpec(
            num_scalar_prefetch=2,
            grid=(slots // GROUP,),
            in_specs=[pl.BlockSpec(s.shape, whole) for s in shards]
            + [pl.BlockSpec((GROUP, block, block), lambda i, m, p: (i, 0, 0))] * split
            + [pl.BlockSpec(tele.shape, whole), pl.BlockSpec(inverse.shape, whole)],
            out_specs=[pl.BlockSpec(s.shape, whole) for s in out_shape],
            scratch_shapes=[
                pltpu.VMEM((parts * blocks + 1, per, block), jnp.bfloat16),
                pltpu.VMEM((blocks, per, block), jnp.float32),
            ],
        ),
        out_shape=out_shape,
        compiler_params=pltpu.CompilerParams(vmem_limit_bytes=32 * MIB),
        cost_estimate=pl.CostEstimate(
            flops=2 * split * slots * block * block * per,
            bytes_accessed=split * slots * block * block * 2,
            transcendentals=0,
        ),
        name="hop",
    )(meta, place, *shards, *tiles, tele, inverse)


def finish_kernel(scale, place, *rest):
    chunks, out, whole = rest[:-2], rest[-2], rest[-1]
    per = chunks[0].shape[0]
    for j, chunk in enumerate(chunks):
        whole[pl.ds(pl.multiple_of((place[0] ^ j) * per, 8), per), :] = chunk[...] * scale
    out[...] = whole[...].T


def finish(place, chunks, scale):
    per, rows = chunks[0].shape
    topics = per * len(chunks)
    return pl.pallas_call(
        functools.partial(finish_kernel, scale),
        in_specs=[pl.BlockSpec(memory_space=pltpu.SMEM)]
        + [pl.BlockSpec(memory_space=pltpu.VMEM)] * len(chunks),
        out_shape=jax.ShapeDtypeStruct((rows, topics), jnp.float32),
        scratch_shapes=[pltpu.VMEM((topics, rows), jnp.float32)],
        compiler_params=pltpu.CompilerParams(vmem_limit_bytes=16 * MIB),
        name="finish",
    )(place, *chunks)


def body(docs, w_in, w_out, doc_host, tiles, dst_block, src_block, tile_count, teleport):
    hosts = teleport.shape[0]
    slots, block, _ = tiles.shape
    parts, split = lax.axis_size("hst"), lax.axis_size("doc")
    blocks = hosts // block
    part = lax.axis_index("hst").astype(jnp.int32)
    place = lax.axis_index("doc").astype(jnp.int32).reshape(1)

    used = jnp.arange(slots, dtype=jnp.int32) < tile_count[0]
    slab = jnp.where(used, src_block ^ (part * blocks), parts * blocks)
    meta = jnp.concatenate([slab, dst_block, jnp.broadcast_to(tile_count, (2 * slots,))])

    def over_doc(value):
        held = {0: value, 1: xor_send(value, "doc", 1)}
        for j in range(2, split, 2):
            held[j] = xor_send(value, "doc", j)
            held[j + 1] = xor_send(held[j], "doc", 1)
        return [held[j] for j in range(split)]

    all_tiles = over_doc(tiles)
    all_meta = jnp.concatenate([meta] + [xor_send(meta, "doc", j) for j in range(1, split)])

    degree = column_sums(meta, tiles, parts, blocks)
    degree = sum(xor_send(degree[j], "hst", j) for j in range(1, parts)) + degree[0]
    degrees = [degree] + [xor_send(degree, "doc", j) for j in range(1, split)]

    sums = document_topics(place, docs, w_in, w_out, doc_host, hosts, split)
    sums = [sums[0]] + [xor_send(sums[j], "doc", j) for j in range(1, split)]

    sent, tele, inverse = start_values(teleport, sums, degrees)
    for step in range(HOPS):
        shards = [sent] + [xor_send(sent, "hst", j) for j in range(1, parts)]
        first, last = step == 0, step == HOPS - 1
        outs = hop(first, last, all_meta, place, shards, all_tiles, tele, inverse)
        sent = outs[0]
        if first:
            tele = outs[1]
    chunks = [outs[0]] + [xor_send(outs[j], "doc", j) for j in range(1, split)]
    return finish(place, chunks, float(hosts * parts))


def solution(mesh):
    placed = (
        P(("hst", "doc"), None),
        P(),
        P(),
        P(("hst", "doc")),
        P(("hst", "doc"), None, None),
        P(("hst", "doc")),
        P(("hst", "doc")),
        P(("hst", "doc")),
        P("hst"),
    )
    return jax.shard_map(
        body, mesh=mesh, in_specs=placed, out_specs=P(("hst", "doc"), None), check_vma=False
    )
```

time: 480 us -> 182 us (0.38)
  waiting for transfers between devices: 337 us -> 80.7 us
  other arithmetic: 58.8 us -> 1.4 us
  starting transfers between devices: 0.48 us -> 53.3 us
  Pallas kernels: 0 us -> 37.5 us
  blocking collectives: 21.4 us -> 0 us
  matrix products: 20.9 us -> 0 us
  local copies, waits for them, and re-layouts: 26.2 us -> 7.16 us
  between operations: 14.5 us -> 0.8 us
    psum x5 -> x0, waiting for transfers between devices: 193 us -> none  [the longest x3 95.5 us: body(): inflow = lax.psum(gathered.reshape(host_dev, topics), 'doc')]
    all_gather x3 -> x0, waiting for transfers between devices: 144 us -> none  [body(): full = lax.all_gather(sent, 'hst', axis=0, tiled=True)]
    ppermute x0 -> x43, waiting for transfers between devices: none -> 80.7 us  [xor_send(): return lax.ppermute(value, axis, [(i, i ^ step) for i in range(size)])]
    ppermute x0 -> x43, starting transfers between devices: none -> 53.3 us  [xor_send(): return lax.ppermute(value, axis, [(i, i ^ step) for i in range(size)])]
    scatter-add x1 -> x0, other arithmetic: 44.5 us -> none  [body(): local_topic = jax.ops.segment_sum(probs, doc_host, num_segments=host_dev)]
    pallas_call x0 -> x7, Pallas kernels: none -> 37.5 us  [the longest x3 23.1 us: hop(): pl.pallas_call(functools.partial(hop_kernel, first, last, parts, split),...]
    psum x1 -> x0, blocking collectives: 21.4 us -> none  [body(): mass = lax.psum(jnp.sum(member[:, None] * host_topic, axis=0), 'hst')]
    dot_general x8 -> x0, matrix products: 20.9 us -> none  [the longest x1 8.62 us: body(): jnp.dot(hidden, w_out, preferred_element_type=jnp.float32)]
  transfers between devices with their start and end apart: 8 -> 43, of which waited for: 8 -> 23; matrix products, arithmetic and copies ran while one was open for 13% -> 1% of each run, Pallas kernels for 0% -> 8%
where the time goes in v1:
time: 182 us; the launch traced here: 181 us
  waiting for transfers between devices  80.7 us (44%)
  starting transfers between devices  53.3 us (29%)
  Pallas kernels  37.5 us (21%)
  local copies, waits for them, and re-layouts  7.16 us (4%)
    ppermute x43, waiting for transfers between devices, xor_send(): return lax.ppermute(value, axis, [(i, i ^ step) for i in range(size)])  80.7 us
    ppermute x43, starting transfers between devices, xor_send(): return lax.ppermute(value, axis, [(i, i ^ step) for i in range(size)])  53.3 us
    pallas_call x3, Pallas kernels, hop(): pl.pallas_call(functools.partial(hop_kernel, first, last, parts, split),...  23.1 us
    pallas_call x1, Pallas kernels, document_topics(): pl.pallas_call(documents_kernel, grid_spec=pltpu.PrefetchScalarGridSpec(n...  13 us
    unnamed x17, local copies, waits for them, and re-layouts  6.3 us
  transfers between devices with their start and end apart: 43, of which 23 were waited for; matrix products, arithmetic and copies ran while one was open for 1% of the time, Pallas kernels for 8%

profile of v1, /device:TPU:0, one launch (start us, length us, event | category | flops | bytes accessed | tf_op | source)
XLA Modules:
  0.0 180.9 jit_solution(18438250955850152434)
XLA Ops:
  0.0 3.0 %collective-permute-start.24 = (bf16[64,128,128]{2,1,0:T(8,128)(2,1)}, bf16[64,128,128]{2,1,0:T(8,128)(2,1)}, u32[]{:S(2)}, u32[]{:S(2)}) collective-permute-start(bf16[64,128,128]{2,1,0:T(8,128)(2,1)} %rest_8_.5), channel_id=1, source_target_pairs={{0,2},{1,3},{2,0},{3,1},{4,6},{5,7},{6,4},{7,5},{8,10},{9,11},{10,... | collective-permute-start | bytes 6291464 | tf_op jit(solution)/shard_map/ppermute | solution.py:21
  3.0 45.9 %collective-permute-done.24.rest_10_ = bf16[64,128,128]{2,1,0:T(8,128)(2,1)} collective-permute-done((bf16[64,128,128]{2,1,0:T(8,128)(2,1)}, bf16[64,128,128]{2,1,0:T(8,128)(2,1)}, u32[]{:S(2)}, u32[]{:S(2)}) %collective-permute-start.24) | collective-permute-done | bytes 2097184 | tf_op jit(solution)/shard_map/ppermute | solution.py:21
  49.6 0.7 compare_select_fusion
  50.2 0.7 pad_add_fusion.meta
  51.0 1.6 copy-done
  52.6 1.2 column_sums.1
  53.7 1.8 collective-permute-start.6
  55.5 1.6 collective-permute-start.7
  57.4 2.8 %collective-permute-start.9 = (f32[16,128]{1,0:T(8,128)S(1)}, f32[16,128]{1,0:T(8,128)S(1)}, u32[]{:S(2)}, u32[]{:S(2)}) collective-permute-start(f32[16,128]{1,0:T(8,128)S(1)} %get-tuple-element.33), channel_id=1, source_target_pairs={{0,16},{4,20},{8,24},{12,28},{16,0},{20,4},{24,8},{28,12},{1,17},{... | collective-permute-start | bytes 24584 | tf_op jit(solution)/shard_map/ppermute | solution.py:21
  60.2 1.5 collective-permute-start.10
  61.7 3.4 %collective-permute-start.11 = (f32[16,128]{1,0:T(8,128)S(1)}, f32[16,128]{1,0:T(8,128)S(1)}, u32[]{:S(2)}, u32[]{:S(2)}) collective-permute-start(f32[16,128]{1,0:T(8,128)S(1)} %get-tuple-element.35), channel_id=1, source_target_pairs={{0,24},{4,28},{8,16},{12,20},{16,8},{20,12},{24,0},{28,4},{1,25},{... | collective-permute-start | bytes 24584 | tf_op jit(solution)/shard_map/ppermute | solution.py:21
  65.1 1.6 collective-permute-start.12
  66.9 0.2 collective-permute-done.11
  67.2 4.3 %collective-permute-done.12 = f32[16,128]{1,0:T(8,128)S(1)} collective-permute-done((f32[16,128]{1,0:T(8,128)S(1)}, f32[16,128]{1,0:T(8,128)S(1)}, u32[]{:S(2)}, u32[]{:S(2)}) %collective-permute-start.12) | collective-permute-done | bytes 8224 | tf_op jit(solution)/shard_map/ppermute | solution.py:21
  71.6 1.5 collective-permute-start.14
  73.1 0.3 collective-permute-start.13
  73.4 4.6 %copy-done.3 = bf16[8192,768]{1,0:T(8,128)(2,1)S(1)} copy-done((bf16[8192,768]{1,0:T(8,128)(2,1)S(1)}, bf16[8192,768]{1,0:T(8,128)(2,1)}, u32[]{:S(2)}) %copy-start.3) | copy-done | bytes 12582936
  78.0 13.0 %document_topics.1 = (f32[16,2048]{1,0:T(8,128)S(1)}, f32[16,2048]{1,0:T(8,128)S(1)}, f32[16,2048]{1,0:T(8,128)S(1)}, f32[16,2048]{1,0:T(8,128)S(1)}) custom-call(s32[1]{0:T(128)} %bitcast.place, bf16[8192,768]{1,0:T(8,128)(2,1)S(1)} %copy-done.3, bf16[768,256]{1,0:T(8,128)(2,1)S(1)} %copy-done.4, bf16[256,64]{1,0:T(8,128)(2,1)S(1)} %copy.10.w_out, ...), custom_call_target="tpu_custom_call" | custom-call | flops 7784628224 | bytes 12582912 | tf_op jit(solution)/shard_map/document_topics/pallas_call | solution.py:111
  91.0 0.3 collective-permute-start.3
  91.3 1.4 collective-permute-start.4
  92.7 0.3 collective-permute-start.5
  93.0 4.7 %collective-permute-done.4.rest_2_ = f32[16,2048]{1,0:T(8,128)S(1)} collective-permute-done((f32[16,2048]{1,0:T(8,128)S(1)}, f32[16,2048]{1,0:T(8,128)S(1)}, u32[]{:S(2)}, u32[]{:S(2)}) %collective-permute-start.4) | collective-permute-done | bytes 131104 | tf_op jit(solution)/shard_map/ppermute | solution.py:21
  97.6 1.6 collective-permute-done.5.rest_3_
  99.4 1.7 collective-permute-start.22
  101.0 1.4 collective-permute-start.2
  102.4 0.5 collective-permute-start.1
  102.9 1.1 collective-permute-done.2
  104.2 1.7 collective-permute-done.1
  105.9 2.1 %collective-permute-start.21 = (bf16[16,2176]{1,0:T(8,128)(2,1)S(1)}, bf16[16,2176]{1,0:T(8,128)(2,1)S(1)}, u32[]{:S(2)}, u32[]{:S(2)}) collective-permute-start(bf16[16,2176]{1,0:T(8,128)(2,1)S(1)} %get-tuple-element.38.rest_0_), channel_id=1, source_target_pairs={{0,24},{4,28},{8,16},{12,20},{16,8},{20,12},{24,0},{28,4},{1,25},{... | collective-permute-start | bytes 208904 | tf_op jit(solution)/shard_map/ppermute | solution.py:21
  108.1 3.8 %collective-permute-start.19 = (bf16[16,2176]{1,0:T(8,128)(2,1)S(1)}, bf16[16,2176]{1,0:T(8,128)(2,1)S(1)}, u32[]{:S(2)}, u32[]{:S(2)}) collective-permute-start(bf16[16,2176]{1,0:T(8,128)(2,1)S(1)} %get-tuple-element.38.rest_0_), channel_id=1, source_target_pairs={{0,16},{4,20},{8,24},{12,28},{16,0},{20,4},{24,8},{28,12},{1,17},{... | collective-permute-start | bytes 208904 | tf_op jit(solution)/shard_map/ppermute | solution.py:21
  111.9 0.4 collective-permute-done.21.rest_6_
  112.3 4.0 %collective-permute-done.20.rest_5_ = bf16[16,2176]{1,0:T(8,128)(2,1)S(1)} collective-permute-done((bf16[16,2176]{1,0:T(8,128)(2,1)S(1)}, bf16[16,2176]{1,0:T(8,128)(2,1)S(1)}, u32[]{:S(2)}, u32[]{:S(2)}) %collective-permute-start.20) | collective-permute-done | bytes 69664 | tf_op jit(solution)/shard_map/ppermute | solution.py:21
  116.3 1.2 collective-permute-done.19.rest_4_
  117.6 0.4 collective-permute-start.16
  118.1 2.5 %collective-permute-done.17.rest_2_ = bf16[16,2176]{1,0:T(8,128)(2,1)S(1)} collective-permute-done((bf16[16,2176]{1,0:T(8,128)(2,1)S(1)}, bf16[16,2176]{1,0:T(8,128)(2,1)S(1)}, u32[]{:S(2)}, u32[]{:S(2)}) %collective-permute-start.17) | collective-permute-done | bytes 69664 | tf_op jit(solution)/shard_map/ppermute | solution.py:21
  120.6 1.2 collective-permute-done.16.rest_1_
  121.9 7.8 %hop.3 = (bf16[16,2048]{1,0:T(8,128)(2,1)S(1)}, f32[16,2048]{1,0:T(8,128)S(1)}) custom-call(s32[1024]{0:T(1024)S(1)} %concatenate.8.meta, s32[1]{0:T(128)} %bitcast.place, bf16[16,2176]{1,0:T(8,128)(2,1)S(1)} %get-tuple-element.38.rest_0_, bf16[16,2176]{1,0:T(8,128)(2,1)S(1)} %collective-permute-done.16.rest_1_, ...), custom_call_target="tpu_custom_call" | custom-call | flops 134217728 | bytes 8388608 | tf_op jit(solution)/shard_map/hop/pallas_call | solution.py:244
  129.7 3.9 %collective-permute-start.32 = (bf16[16,2048]{1,0:T(8,128)(2,1)S(1)}, bf16[16,2048]{1,0:T(8,128)(2,1)S(1)}, u32[]{:S(2)}, u32[]{:S(2)}) collective-permute-start(bf16[16,2048]{1,0:T(8,128)(2,1)S(1)} %get-tuple-element.41.rest_0_), channel_id=1, source_target_pairs={{0,28},{4,24},{8,20},{12,16},{16,12},{20,8},{24,4},{28,0},{1,29},{... | collective-permute-start | bytes 196616 | tf_op jit(solution)/shard_map/ppermute | solution.py:21
  133.5 0.7 collective-permute-start.30
  134.2 3.2 %collective-permute-start.29 = (bf16[16,2048]{1,0:T(8,128)(2,1)S(1)}, bf16[16,2048]{1,0:T(8,128)(2,1)S(1)}, u32[]{:S(2)}, u32[]{:S(2)}) collective-permute-start(bf16[16,2048]{1,0:T(8,128)(2,1)S(1)} %get-tuple-element.41.rest_0_), channel_id=1, source_target_pairs={{0,16},{4,20},{8,24},{12,28},{16,0},{20,4},{24,8},{28,12},{1,17},{... | collective-permute-start | bytes 196616 | tf_op jit(solution)/shard_map/ppermute | solution.py:21
  137.4 1.4 collective-permute-start.28
  138.8 0.6 collective-permute-start.27
  139.4 0.7 collective-permute-done.31.rest_6_
  140.1 0.8 collective-permute-start.26
  140.9 1.8 collective-permute-done.30.rest_5_
  142.6 1.3 collective-permute-done.29.rest_4_
  143.9 0.7 collective-permute-done.27.rest_2_
  144.6 7.7 %hop.4.rest_0_ = bf16[16,2048]{1,0:T(8,128)(2,1)S(1)} custom-call(s32[1024]{0:T(1024)S(1)} %concatenate.8.meta, s32[1]{0:T(128)} %bitcast.place, bf16[16,2048]{1,0:T(8,128)(2,1)S(1)} %get-tuple-element.41.rest_0_, bf16[16,2048]{1,0:T(8,128)(2,1)S(1)} %collective-permute-done.26.rest_1_, bf16[16,2048]{1,0:T(8,128)(2,1)S(1)} %collective-permute-done.27.rest_2_, ...), custom_call_target="tpu_custom_call" | custom-call | flops 134217728 | bytes 8388608 | tf_op jit(solution)/shard_map/hop/pallas_call | solution.py:244
  152.3 4.1 %collective-permute-start.39 = (bf16[16,2048]{1,0:T(8,128)(2,1)S(1)}, bf16[16,2048]{1,0:T(8,128)(2,1)S(1)}, u32[]{:S(2)}, u32[]{:S(2)}) collective-permute-start(bf16[16,2048]{1,0:T(8,128)(2,1)S(1)} %hop.4.rest_0_), channel_id=1, source_target_pairs={{0,28},{4,24},{8,20},{12,16},{16,12},{20,8},{24,4},{28,0},{1,29},{... | collective-permute-start | bytes 196616 | tf_op jit(solution)/shard_map/ppermute | solution.py:21
  156.4 0.5 collective-permute-start.37
  156.9 3.1 %collective-permute-start.36 = (bf16[16,2048]{1,0:T(8,128)(2,1)S(1)}, bf16[16,2048]{1,0:T(8,128)(2,1)S(1)}, u32[]{:S(2)}, u32[]{:S(2)}) collective-permute-start(bf16[16,2048]{1,0:T(8,128)(2,1)S(1)} %hop.4.rest_0_), channel_id=1, source_target_pairs={{0,16},{4,20},{8,24},{12,28},{16,0},{20,4},{24,8},{28,12},{1,17},{... | collective-permute-start | bytes 196616 | tf_op jit(solution)/shard_map/ppermute | solution.py:21
  160.0 1.6 collective-permute-start.35
  161.7 0.6 collective-permute-start.34
  162.2 0.4 collective-permute-done.38.rest_6_
  162.6 1.2 collective-permute-start.33
  163.8 1.7 collective-permute-done.37.rest_5_
  165.5 1.4 collective-permute-done.36.rest_4_
  166.9 0.6 collective-permute-done.34.rest_2_
  167.5 7.7 %hop.5 = (f32[16,512]{1,0:T(8,128)S(1)}, f32[16,512]{1,0:T(8,128)S(1)}, f32[16,512]{1,0:T(8,128)S(1)}, f32[16,512]{1,0:T(8,128)S(1)}) custom-call(s32[1024]{0:T(1024)S(1)} %concatenate.8.meta, s32[1]{0:T(128)} %bitcast.place, bf16[16,2048]{1,0:T(8,128)(2,1)S(1)} %hop.4.rest_0_, bf16[16,2048]{1,0:T(8,128)(2,1)S(1)} %collective-permute-done.33.rest_1_, ...), custom_call_target="tpu_custom_call" | custom-call | flops 134217728 | bytes 8388608 | tf_op jit(solution)/shard_map/hop/pallas_call | solution.py:244
  175.2 1.4 collective-permute-start.41
  176.6 0.5 collective-permute-start.42
  177.1 2.1 %collective-permute-done.41.rest_2_ = f32[16,512]{1,0:T(8,128)S(1)} collective-permute-done((f32[16,512]{1,0:T(8,128)S(1)}, f32[16,512]{1,0:T(8,128)S(1)}, u32[]{:S(2)}, u32[]{:S(2)}) %collective-permute-start.41) | collective-permute-done | bytes 32800 | tf_op jit(solution)/shard_map/ppermute | solution.py:21
  179.2 0.7 collective-permute-done.42.rest_3_
  180.1 0.8 copy.11
  (52 shorter events, 1.3 us)
Async XLA Ops:
  0.0 48.9 %collective-permute-start.24 = (bf16[64,128,128]{2,1,0:T(8,128)(2,1)}, bf16[64,128,128]{2,1,0:T(8,128)(2,1)}, u32[]{:S(2)}, u32[]{:S(2)}) collective-permute-start(bf16[64,128,128]{2,1,0:T(8,128)(2,1)} %rest_8_.5), channel_id=1, source_target_pairs={{0,2},{1,3},{2,0},{3,1},{4,6},{5,7},{6,4},{7,5},{8,10},{9,11},{10,... | collective-permute-start | bytes 6291464 | tf_op jit(solution)/shard_map/ppermute | solution.py:21
  3.0 118.9 %collective-permute-start.23 = (bf16[64,128,128]{2,1,0:T(8,128)(2,1)}, bf16[64,128,128]{2,1,0:T(8,128)(2,1)}, u32[]{:S(2)}, u32[]{:S(2)}) collective-permute-start(bf16[64,128,128]{2,1,0:T(8,128)(2,1)} %rest_8_.5), channel_id=1, source_target_pairs={{0,1},{1,0},{2,3},{3,2},{4,5},{5,4},{6,7},{7,6},{8,9},{9,8},{10,11... | collective-permute-start | bytes 6291464 | tf_op jit(solution)/shard_map/ppermute | solution.py:21
  48.9 73.0 %collective-permute-start.25 = (bf16[64,128,128]{2,1,0:T(8,128)(2,1)}, bf16[64,128,128]{2,1,0:T(8,128)(2,1)}, u32[]{:S(2)}, u32[]{:S(2)}) collective-permute-start(bf16[64,128,128]{2,1,0:T(8,128)(2,1)} %collective-permute-done.24.rest_10_), channel_id=1, source_target_pairs={{0,1},{1,0},{2,3},{3,2},{4,5},{5,4},{6,7},{7,6},{8,9},{9,8},{10,11... | collective-permute-start | bytes 6291464 | tf_op jit(solution)/shard_map/ppermute | solution.py:21
  51.0 1.6 copy-start
  52.6 14.2 %copy-start.6 = (bf16[256,64]{0,1:T(8,128)(2,1)S(1)}, bf16[256,64]{0,1:T(8,128)(2,1)}, u32[]{:S(2)}) copy-start(bf16[256,64]{0,1:T(8,128)(2,1)} %param.11) | copy-start | bytes 98308
  52.6 20.9 %copy-start.4 = (bf16[768,256]{1,0:T(8,128)(2,1)S(1)}, bf16[768,256]{1,0:T(8,128)(2,1)}, u32[]{:S(2)}) copy-start(bf16[768,256]{1,0:T(8,128)(2,1)} %w_in.1) | copy-start | bytes 1179652
  52.6 20.9 %copy-start.5 = (s32[8192]{0:T(1024)S(1)}, s32[8192]{0:T(1024)}, u32[]{:S(2)}) copy-start(s32[8192]{0:T(1024)} %param.12) | copy-start | bytes 98308
  53.7 3.7 %collective-permute-start.6 = (f32[16,128]{1,0:T(8,128)S(1)}, f32[16,128]{1,0:T(8,128)S(1)}, u32[]{:S(2)}, u32[]{:S(2)}) collective-permute-start(f32[16,128]{1,0:T(8,128)S(1)} %get-tuple-element.30), channel_id=1, source_target_pairs={{0,4},{4,0},{8,12},{12,8},{16,20},{20,16},{24,28},{28,24},{1,5},{5... | collective-permute-start | bytes 24584 | tf_op jit(solution)/shard_map/ppermute | solution.py:21
  55.5 4.7 %collective-permute-start.7 = (f32[16,128]{1,0:T(8,128)S(1)}, f32[16,128]{1,0:T(8,128)S(1)}, u32[]{:S(2)}, u32[]{:S(2)}) collective-permute-start(f32[16,128]{1,0:T(8,128)S(1)} %get-tuple-element.31), channel_id=1, source_target_pairs={{0,8},{4,12},{8,0},{12,4},{16,24},{20,28},{24,16},{28,20},{1,9},{5... | collective-permute-start | bytes 24584 | tf_op jit(solution)/shard_map/ppermute | solution.py:21
  57.1 4.6 %collective-permute-start.8 = (f32[16,128]{1,0:T(8,128)S(1)}, f32[16,128]{1,0:T(8,128)S(1)}, u32[]{:S(2)}, u32[]{:S(2)}) collective-permute-start(f32[16,128]{1,0:T(8,128)S(1)} %get-tuple-element.32), channel_id=1, source_target_pairs={{0,12},{4,8},{8,4},{12,0},{16,28},{20,24},{24,20},{28,16},{1,13},{... | collective-permute-start | bytes 24584 | tf_op jit(solution)/shard_map/ppermute | solution.py:21
  57.4 7.7 %collective-permute-start.9 = (f32[16,128]{1,0:T(8,128)S(1)}, f32[16,128]{1,0:T(8,128)S(1)}, u32[]{:S(2)}, u32[]{:S(2)}) collective-permute-start(f32[16,128]{1,0:T(8,128)S(1)} %get-tuple-element.33), channel_id=1, source_target_pairs={{0,16},{4,20},{8,24},{12,28},{16,0},{20,4},{24,8},{28,12},{1,17},{... | collective-permute-start | bytes 24584 | tf_op jit(solution)/shard_map/ppermute | solution.py:21
  60.2 6.7 %collective-permute-start.10 = (f32[16,128]{1,0:T(8,128)S(1)}, f32[16,128]{1,0:T(8,128)S(1)}, u32[]{:S(2)}, u32[]{:S(2)}) collective-permute-start(f32[16,128]{1,0:T(8,128)S(1)} %get-tuple-element.34), channel_id=1, source_target_pairs={{0,20},{4,16},{8,28},{12,24},{16,4},{20,0},{24,12},{28,8},{1,21},{... | collective-permute-start | bytes 24584 | tf_op jit(solution)/shard_map/ppermute | solution.py:21
  61.7 5.4 %collective-permute-start.11 = (f32[16,128]{1,0:T(8,128)S(1)}, f32[16,128]{1,0:T(8,128)S(1)}, u32[]{:S(2)}, u32[]{:S(2)}) collective-permute-start(f32[16,128]{1,0:T(8,128)S(1)} %get-tuple-element.35), channel_id=1, source_target_pairs={{0,24},{4,28},{8,16},{12,20},{16,8},{20,12},{24,0},{28,4},{1,25},{... | collective-permute-start | bytes 24584 | tf_op jit(solution)/shard_map/ppermute | solution.py:21
  65.1 6.3 %collective-permute-start.12 = (f32[16,128]{1,0:T(8,128)S(1)}, f32[16,128]{1,0:T(8,128)S(1)}, u32[]{:S(2)}, u32[]{:S(2)}) collective-permute-start(f32[16,128]{1,0:T(8,128)S(1)} %get-tuple-element.36), channel_id=1, source_target_pairs={{0,28},{4,24},{8,20},{12,16},{16,12},{20,8},{24,4},{28,0},{1,29},{... | collective-permute-start | bytes 24584 | tf_op jit(solution)/shard_map/ppermute | solution.py:21
  71.5 19.5 %collective-permute-start.15 = (f32[16,128]{1,0:T(8,128)S(1)}, f32[16,128]{1,0:T(8,128)S(1)}, u32[]{:S(2)}, u32[]{:S(2)}) collective-permute-start(f32[16,128]{1,0:T(8,128)S(1)} %add_add_fusion.rest_4_), channel_id=1, source_target_pairs={{0,3},{1,2},{2,1},{3,0},{4,7},{5,6},{6,5},{7,4},{8,11},{9,10},{10,... | collective-permute-start | bytes 24584 | tf_op jit(solution)/shard_map/ppermute | solution.py:21
  71.6 19.7 %collective-permute-start.14 = (f32[16,128]{1,0:T(8,128)S(1)}, f32[16,128]{1,0:T(8,128)S(1)}, u32[]{:S(2)}, u32[]{:S(2)}) collective-permute-start(f32[16,128]{1,0:T(8,128)S(1)} %add_add_fusion.rest_4_), channel_id=1, source_target_pairs={{0,2},{1,3},{2,0},{3,1},{4,6},{5,7},{6,4},{7,5},{8,10},{9,11},{10,... | collective-permute-start | bytes 24584 | tf_op jit(solution)/shard_map/ppermute | solution.py:21
  73.1 19.6 %collective-permute-start.13 = (f32[16,128]{1,0:T(8,128)S(1)}, f32[16,128]{1,0:T(8,128)S(1)}, u32[]{:S(2)}, u32[]{:S(2)}) collective-permute-start(f32[16,128]{1,0:T(8,128)S(1)} %add_add_fusion.rest_4_), channel_id=1, source_target_pairs={{0,1},{1,0},{2,3},{3,2},{4,5},{5,4},{6,7},{7,6},{8,9},{9,8},{10,11... | collective-permute-start | bytes 24584 | tf_op jit(solution)/shard_map/ppermute | solution.py:21
  73.4 4.6 %copy-start.3 = (bf16[8192,768]{1,0:T(8,128)(2,1)S(1)}, bf16[8192,768]{1,0:T(8,128)(2,1)}, u32[]{:S(2)}) copy-start(bf16[8192,768]{1,0:T(8,128)(2,1)} %docs.1) | copy-start | bytes 37748740
  78.0 21.2 %copy-start.2 = (s32[2048]{0:T(1024)S(1)}, s32[2048]{0:T(1024)}, u32[]{:S(2)}) copy-start(s32[2048]{0:T(1024)} %param.17) | copy-start | bytes 24580
  78.0 40.0 %copy-start.7 = (s32[64]{0:T(128)S(1)}, s32[64]{0:T(128)}, u32[]{:S(2)}) copy-start(s32[64]{0:T(128)} %param.14) | copy-start | bytes 772
  78.0 43.9 %copy-start.1 = (bf16[64,128,128]{2,1,0:T(8,128)(2,1)S(1)}, bf16[64,128,128]{2,1,0:T(8,128)(2,1)}, u32[]{:S(2)}) copy-start(bf16[64,128,128]{2,1,0:T(8,128)(2,1)} %rest_8_.5) | copy-start | bytes 6291460
  91.0 1.9 %collective-permute-start.3 = (f32[16,2048]{1,0:T(8,128)S(1)}, f32[16,2048]{1,0:T(8,128)S(1)}, u32[]{:S(2)}, u32[]{:S(2)}) collective-permute-start(f32[16,2048]{1,0:T(8,128)S(1)} %get-tuple-element.27), channel_id=1, source_target_pairs={{0,1},{1,0},{2,3},{3,2},{4,5},{5,4},{6,7},{7,6},{8,9},{9,8},{10,11... | collective-permute-start | bytes 393224 | tf_op jit(solution)/shard_map/ppermute | solution.py:21
  91.3 6.3 %collective-permute-start.4 = (f32[16,2048]{1,0:T(8,128)S(1)}, f32[16,2048]{1,0:T(8,128)S(1)}, u32[]{:S(2)}, u32[]{:S(2)}) collective-permute-start(f32[16,2048]{1,0:T(8,128)S(1)} %get-tuple-element.28), channel_id=1, source_target_pairs={{0,2},{1,3},{2,0},{3,1},{4,6},{5,7},{6,4},{7,5},{8,10},{9,11},{10,... | collective-permute-start | bytes 393224 | tf_op jit(solution)/shard_map/ppermute | solution.py:21
  92.7 6.5 %collective-permute-start.5 = (f32[16,2048]{1,0:T(8,128)S(1)}, f32[16,2048]{1,0:T(8,128)S(1)}, u32[]{:S(2)}, u32[]{:S(2)}) collective-permute-start(f32[16,2048]{1,0:T(8,128)S(1)} %get-tuple-element.29), channel_id=1, source_target_pairs={{0,3},{1,2},{2,1},{3,0},{4,7},{5,6},{6,5},{7,4},{8,11},{9,10},{10,... | collective-permute-start | bytes 393224 | tf_op jit(solution)/shard_map/ppermute | solution.py:21
  99.4 8.7 %collective-permute-start.22 = (bf16[16,2176]{1,0:T(8,128)(2,1)S(1)}, bf16[16,2176]{1,0:T(8,128)(2,1)S(1)}, u32[]{:S(2)}, u32[]{:S(2)}) collective-permute-start(bf16[16,2176]{1,0:T(8,128)(2,1)S(1)} %get-tuple-element.38.rest_0_), channel_id=1, source_target_pairs={{0,28},{4,24},{8,20},{12,16},{16,12},{20,8},{24,4},{28,0},{1,29},{... | collective-permute-start | bytes 208904 | tf_op jit(solution)/shard_map/ppermute | solution.py:21
  101.0 3.0 %collective-permute-start.2 = (s32[256]{0:T(256)S(1)}, s32[256]{0:T(256)S(1)}, u32[]{:S(2)}, u32[]{:S(2)}) collective-permute-start(s32[256]{0:T(256)S(1)} %pad_add_fusion.meta), channel_id=1, source_target_pairs={{0,3},{1,2},{2,1},{3,0},{4,7},{5,6},{6,5},{7,4},{8,11},{9,10},{10,... | collective-permute-start | bytes 3080 | tf_op jit(solution)/shard_map/ppermute | solution.py:21
  102.4 3.6 %collective-permute-start.1 = (s32[256]{0:T(256)S(1)}, s32[256]{0:T(256)S(1)}, u32[]{:S(2)}, u32[]{:S(2)}) collective-permute-start(s32[256]{0:T(256)S(1)} %pad_add_fusion.meta), channel_id=1, source_target_pairs={{0,2},{1,3},{2,0},{3,1},{4,6},{5,7},{6,4},{7,5},{8,10},{9,11},{10,... | collective-permute-start | bytes 3080 | tf_op jit(solution)/shard_map/ppermute | solution.py:21
  104.0 4.1 %collective-permute-start = (s32[256]{0:T(256)S(1)}, s32[256]{0:T(256)S(1)}, u32[]{:S(2)}, u32[]{:S(2)}) collective-permute-start(s32[256]{0:T(256)S(1)} %pad_add_fusion.meta), channel_id=1, source_target_pairs={{0,1},{1,0},{2,3},{3,2},{4,5},{5,4},{6,7},{7,6},{8,9},{9,8},{10,11... | collective-permute-start | bytes 3080 | tf_op jit(solution)/shard_map/ppermute | solution.py:21
  105.9 6.4 %collective-permute-start.21 = (bf16[16,2176]{1,0:T(8,128)(2,1)S(1)}, bf16[16,2176]{1,0:T(8,128)(2,1)S(1)}, u32[]{:S(2)}, u32[]{:S(2)}) collective-permute-start(bf16[16,2176]{1,0:T(8,128)(2,1)S(1)} %get-tuple-element.38.rest_0_), channel_id=1, source_target_pairs={{0,24},{4,28},{8,16},{12,20},{16,8},{20,12},{24,0},{28,4},{1,25},{... | collective-permute-start | bytes 208904 | tf_op jit(solution)/shard_map/ppermute | solution.py:21
  108.1 8.3 %collective-permute-start.20 = (bf16[16,2176]{1,0:T(8,128)(2,1)S(1)}, bf16[16,2176]{1,0:T(8,128)(2,1)S(1)}, u32[]{:S(2)}, u32[]{:S(2)}) collective-permute-start(bf16[16,2176]{1,0:T(8,128)(2,1)S(1)} %get-tuple-element.38.rest_0_), channel_id=1, source_target_pairs={{0,20},{4,16},{8,28},{12,24},{16,4},{20,0},{24,12},{28,8},{1,21},{... | collective-permute-start | bytes 208904 | tf_op jit(solution)/shard_map/ppermute | solution.py:21
  108.1 9.5 %collective-permute-start.19 = (bf16[16,2176]{1,0:T(8,128)(2,1)S(1)}, bf16[16,2176]{1,0:T(8,128)(2,1)S(1)}, u32[]{:S(2)}, u32[]{:S(2)}) collective-permute-start(bf16[16,2176]{1,0:T(8,128)(2,1)S(1)} %get-tuple-element.38.rest_0_), channel_id=1, source_target_pairs={{0,16},{4,20},{8,24},{12,28},{16,0},{20,4},{24,8},{28,12},{1,17},{... | collective-permute-start | bytes 208904 | tf_op jit(solution)/shard_map/ppermute | solution.py:21
  112.3 5.8 %collective-permute-start.18 = (bf16[16,2176]{1,0:T(8,128)(2,1)S(1)}, bf16[16,2176]{1,0:T(8,128)(2,1)S(1)}, u32[]{:S(2)}, u32[]{:S(2)}) collective-permute-start(bf16[16,2176]{1,0:T(8,128)(2,1)S(1)} %get-tuple-element.38.rest_0_), channel_id=1, source_target_pairs={{0,12},{4,8},{8,4},{12,0},{16,28},{20,24},{24,20},{28,16},{1,13},{... | collective-permute-start | bytes 208904 | tf_op jit(solution)/shard_map/ppermute | solution.py:21
  116.3 4.3 %collective-permute-start.17 = (bf16[16,2176]{1,0:T(8,128)(2,1)S(1)}, bf16[16,2176]{1,0:T(8,128)(2,1)S(1)}, u32[]{:S(2)}, u32[]{:S(2)}) collective-permute-start(bf16[16,2176]{1,0:T(8,128)(2,1)S(1)} %get-tuple-element.38.rest_0_), channel_id=1, source_target_pairs={{0,8},{4,12},{8,0},{12,4},{16,24},{20,28},{24,16},{28,20},{1,9},{5... | collective-permute-start | bytes 208904 | tf_op jit(solution)/shard_map/ppermute | solution.py:21
  117.6 4.3 %collective-permute-start.16 = (bf16[16,2176]{1,0:T(8,128)(2,1)S(1)}, bf16[16,2176]{1,0:T(8,128)(2,1)S(1)}, u32[]{:S(2)}, u32[]{:S(2)}) collective-permute-start(bf16[16,2176]{1,0:T(8,128)(2,1)S(1)} %get-tuple-element.38.rest_0_), channel_id=1, source_target_pairs={{0,4},{4,0},{8,12},{12,8},{16,20},{20,16},{24,28},{28,24},{1,5},{5... | collective-permute-start | bytes 208904 | tf_op jit(solution)/shard_map/ppermute | solution.py:21
  129.7 9.2 %collective-permute-start.32 = (bf16[16,2048]{1,0:T(8,128)(2,1)S(1)}, bf16[16,2048]{1,0:T(8,128)(2,1)S(1)}, u32[]{:S(2)}, u32[]{:S(2)}) collective-permute-start(bf16[16,2048]{1,0:T(8,128)(2,1)S(1)} %get-tuple-element.41.rest_0_), channel_id=1, source_target_pairs={{0,28},{4,24},{8,20},{12,16},{16,12},{20,8},{24,4},{28,0},{1,29},{... | collective-permute-start | bytes 196616 | tf_op jit(solution)/shard_map/ppermute | solution.py:21
  133.5 6.6 %collective-permute-start.31 = (bf16[16,2048]{1,0:T(8,128)(2,1)S(1)}, bf16[16,2048]{1,0:T(8,128)(2,1)S(1)}, u32[]{:S(2)}, u32[]{:S(2)}) collective-permute-start(bf16[16,2048]{1,0:T(8,128)(2,1)S(1)} %get-tuple-element.41.rest_0_), channel_id=1, source_target_pairs={{0,24},{4,28},{8,16},{12,20},{16,8},{20,12},{24,0},{28,4},{1,25},{... | collective-permute-start | bytes 196616 | tf_op jit(solution)/shard_map/ppermute | solution.py:21
  133.5 9.1 %collective-permute-start.30 = (bf16[16,2048]{1,0:T(8,128)(2,1)S(1)}, bf16[16,2048]{1,0:T(8,128)(2,1)S(1)}, u32[]{:S(2)}, u32[]{:S(2)}) collective-permute-start(bf16[16,2048]{1,0:T(8,128)(2,1)S(1)} %get-tuple-element.41.rest_0_), channel_id=1, source_target_pairs={{0,20},{4,16},{8,28},{12,24},{16,4},{20,0},{24,12},{28,8},{1,21},{... | collective-permute-start | bytes 196616 | tf_op jit(solution)/shard_map/ppermute | solution.py:21
  134.2 9.7 %collective-permute-start.29 = (bf16[16,2048]{1,0:T(8,128)(2,1)S(1)}, bf16[16,2048]{1,0:T(8,128)(2,1)S(1)}, u32[]{:S(2)}, u32[]{:S(2)}) collective-permute-start(bf16[16,2048]{1,0:T(8,128)(2,1)S(1)} %get-tuple-element.41.rest_0_), channel_id=1, source_target_pairs={{0,16},{4,20},{8,24},{12,28},{16,0},{20,4},{24,8},{28,12},{1,17},{... | collective-permute-start | bytes 196616 | tf_op jit(solution)/shard_map/ppermute | solution.py:21
  137.4 6.6 %collective-permute-start.28 = (bf16[16,2048]{1,0:T(8,128)(2,1)S(1)}, bf16[16,2048]{1,0:T(8,128)(2,1)S(1)}, u32[]{:S(2)}, u32[]{:S(2)}) collective-permute-start(bf16[16,2048]{1,0:T(8,128)(2,1)S(1)} %get-tuple-element.41.rest_0_), channel_id=1, source_target_pairs={{0,12},{4,8},{8,4},{12,0},{16,28},{20,24},{24,20},{28,16},{1,13},{... | collective-permute-start | bytes 196616 | tf_op jit(solution)/shard_map/ppermute | solution.py:21
  138.8 5.8 %collective-permute-start.27 = (bf16[16,2048]{1,0:T(8,128)(2,1)S(1)}, bf16[16,2048]{1,0:T(8,128)(2,1)S(1)}, u32[]{:S(2)}, u32[]{:S(2)}) collective-permute-start(bf16[16,2048]{1,0:T(8,128)(2,1)S(1)} %get-tuple-element.41.rest_0_), channel_id=1, source_target_pairs={{0,8},{4,12},{8,0},{12,4},{16,24},{20,28},{24,16},{28,20},{1,9},{5... | collective-permute-start | bytes 196616 | tf_op jit(solution)/shard_map/ppermute | solution.py:21
  140.1 4.5 %collective-permute-start.26 = (bf16[16,2048]{1,0:T(8,128)(2,1)S(1)}, bf16[16,2048]{1,0:T(8,128)(2,1)S(1)}, u32[]{:S(2)}, u32[]{:S(2)}) collective-permute-start(bf16[16,2048]{1,0:T(8,128)(2,1)S(1)} %get-tuple-element.41.rest_0_), channel_id=1, source_target_pairs={{0,4},{4,0},{8,12},{12,8},{16,20},{20,16},{24,28},{28,24},{1,5},{5... | collective-permute-start | bytes 196616 | tf_op jit(solution)/shard_map/ppermute | solution.py:21
  152.3 9.4 %collective-permute-start.39 = (bf16[16,2048]{1,0:T(8,128)(2,1)S(1)}, bf16[16,2048]{1,0:T(8,128)(2,1)S(1)}, u32[]{:S(2)}, u32[]{:S(2)}) collective-permute-start(bf16[16,2048]{1,0:T(8,128)(2,1)S(1)} %hop.4.rest_0_), channel_id=1, source_target_pairs={{0,28},{4,24},{8,20},{12,16},{16,12},{20,8},{24,4},{28,0},{1,29},{... | collective-permute-start | bytes 196616 | tf_op jit(solution)/shard_map/ppermute | solution.py:21
  156.4 6.2 %collective-permute-start.38 = (bf16[16,2048]{1,0:T(8,128)(2,1)S(1)}, bf16[16,2048]{1,0:T(8,128)(2,1)S(1)}, u32[]{:S(2)}, u32[]{:S(2)}) collective-permute-start(bf16[16,2048]{1,0:T(8,128)(2,1)S(1)} %hop.4.rest_0_), channel_id=1, source_target_pairs={{0,24},{4,28},{8,16},{12,20},{16,8},{20,12},{24,0},{28,4},{1,25},{... | collective-permute-start | bytes 196616 | tf_op jit(solution)/shard_map/ppermute | solution.py:21
  156.4 9.1 %collective-permute-start.37 = (bf16[16,2048]{1,0:T(8,128)(2,1)S(1)}, bf16[16,2048]{1,0:T(8,128)(2,1)S(1)}, u32[]{:S(2)}, u32[]{:S(2)}) collective-permute-start(bf16[16,2048]{1,0:T(8,128)(2,1)S(1)} %hop.4.rest_0_), channel_id=1, source_target_pairs={{0,20},{4,16},{8,28},{12,24},{16,4},{20,0},{24,12},{28,8},{1,21},{... | collective-permute-start | bytes 196616 | tf_op jit(solution)/shard_map/ppermute | solution.py:21
  156.9 10.0 %collective-permute-start.36 = (bf16[16,2048]{1,0:T(8,128)(2,1)S(1)}, bf16[16,2048]{1,0:T(8,128)(2,1)S(1)}, u32[]{:S(2)}, u32[]{:S(2)}) collective-permute-start(bf16[16,2048]{1,0:T(8,128)(2,1)S(1)} %hop.4.rest_0_), channel_id=1, source_target_pairs={{0,16},{4,20},{8,24},{12,28},{16,0},{20,4},{24,8},{28,12},{1,17},{... | collective-permute-start | bytes 196616 | tf_op jit(solution)/shard_map/ppermute | solution.py:21
  160.0 6.9 %collective-permute-start.35 = (bf16[16,2048]{1,0:T(8,128)(2,1)S(1)}, bf16[16,2048]{1,0:T(8,128)(2,1)S(1)}, u32[]{:S(2)}, u32[]{:S(2)}) collective-permute-start(bf16[16,2048]{1,0:T(8,128)(2,1)S(1)} %hop.4.rest_0_), channel_id=1, source_target_pairs={{0,12},{4,8},{8,4},{12,0},{16,28},{20,24},{24,20},{28,16},{1,13},{... | collective-permute-start | bytes 196616 | tf_op jit(solution)/shard_map/ppermute | solution.py:21
  161.7 5.8 %collective-permute-start.34 = (bf16[16,2048]{1,0:T(8,128)(2,1)S(1)}, bf16[16,2048]{1,0:T(8,128)(2,1)S(1)}, u32[]{:S(2)}, u32[]{:S(2)}) collective-permute-start(bf16[16,2048]{1,0:T(8,128)(2,1)S(1)} %hop.4.rest_0_), channel_id=1, source_target_pairs={{0,8},{4,12},{8,0},{12,4},{16,24},{20,28},{24,16},{28,20},{1,9},{5... | collective-permute-start | bytes 196616 | tf_op jit(solution)/shard_map/ppermute | solution.py:21
  162.6 4.9 %collective-permute-start.33 = (bf16[16,2048]{1,0:T(8,128)(2,1)S(1)}, bf16[16,2048]{1,0:T(8,128)(2,1)S(1)}, u32[]{:S(2)}, u32[]{:S(2)}) collective-permute-start(bf16[16,2048]{1,0:T(8,128)(2,1)S(1)} %hop.4.rest_0_), channel_id=1, source_target_pairs={{0,4},{4,0},{8,12},{12,8},{16,20},{20,16},{24,28},{28,24},{1,5},{5... | collective-permute-start | bytes 196616 | tf_op jit(solution)/shard_map/ppermute | solution.py:21
  175.1 1.9 %collective-permute-start.40 = (f32[16,512]{1,0:T(8,128)S(1)}, f32[16,512]{1,0:T(8,128)S(1)}, u32[]{:S(2)}, u32[]{:S(2)}) collective-permute-start(f32[16,512]{1,0:T(8,128)S(1)} %get-tuple-element.44), channel_id=1, source_target_pairs={{0,1},{1,0},{2,3},{3,2},{4,5},{5,4},{6,7},{7,6},{8,9},{9,8},{10,11... | collective-permute-start | bytes 98312 | tf_op jit(solution)/shard_map/ppermute | solution.py:21
  175.2 4.0 %collective-permute-start.41 = (f32[16,512]{1,0:T(8,128)S(1)}, f32[16,512]{1,0:T(8,128)S(1)}, u32[]{:S(2)}, u32[]{:S(2)}) collective-permute-start(f32[16,512]{1,0:T(8,128)S(1)} %get-tuple-element.45), channel_id=1, source_target_pairs={{0,2},{1,3},{2,0},{3,1},{4,6},{5,7},{6,4},{7,5},{8,10},{9,11},{10,... | collective-permute-start | bytes 98312 | tf_op jit(solution)/shard_map/ppermute | solution.py:21
  176.6 3.3 %collective-permute-start.42 = (f32[16,512]{1,0:T(8,128)S(1)}, f32[16,512]{1,0:T(8,128)S(1)}, u32[]{:S(2)}, u32[]{:S(2)}) collective-permute-start(f32[16,512]{1,0:T(8,128)S(1)} %get-tuple-element.46), channel_id=1, source_target_pairs={{0,3},{1,2},{2,1},{3,0},{4,7},{5,6},{6,5},{7,4},{8,11},{9,10},{10,... | collective-permute-start | bytes 98312 | tf_op jit(solution)/shard_map/ppermute | solution.py:21

commit v2 on v1

v2 whole, which is shorter than its diff:
```python
import functools

import jax
import jax.numpy as jnp
from jax import lax
from jax.experimental import pallas as pl
from jax.experimental.pallas import tpu as pltpu
from jax.sharding import PartitionSpec as P

HOPS = 3
DIGITS = 4
DOC_BLOCK = 1024
GROUP = 8
TILE_GROUP = 16
LIFT = 2.0**64
NT = (((1,), (1,)), ((), ()))
MIB = 1 << 20


def xor_send(value, axis, step):
    size = lax.axis_size(axis)
    return lax.ppermute(value, axis, [(i, i ^ step) for i in range(size)])


def column_sum_kernel(meta, tiles, out, total):
    step = pl.program_id(0)

    @pl.when(step == 0)
    def _():
        total[...] = jnp.zeros_like(total)

    for i in range(GROUP):
        row = meta[step * GROUP + i]
        part = jnp.sum(tiles[i].astype(jnp.float32), axis=0, keepdims=True)
        total[pl.ds(row, 1), :] += part

    @pl.when(step == pl.num_programs(0) - 1)
    def _():
        rows = out.shape[1]
        for j in range(out.shape[0]):
            out[j] = total[j * rows : (j + 1) * rows, :]


def column_sums(meta, tiles, parts, rows):
    slots, block, _ = tiles.shape
    shape = (parts, rows, block)
    return pl.pallas_call(
        column_sum_kernel,
        grid_spec=pltpu.PrefetchScalarGridSpec(
            num_scalar_prefetch=1,
            grid=(slots // GROUP,),
            in_specs=[pl.BlockSpec((GROUP, block, block), lambda i, m: (i, 0, 0))],
            out_specs=pl.BlockSpec(shape, lambda i, m: (0, 0, 0)),
            scratch_shapes=[pltpu.VMEM((parts * rows + 8, block), jnp.float32)],
        ),
        out_shape=jax.ShapeDtypeStruct(shape, jnp.float32),
        compiler_params=pltpu.CompilerParams(vmem_limit_bytes=16 * MIB),
        cost_estimate=pl.CostEstimate(
            flops=tiles.size, bytes_accessed=tiles.size * 2, transcendentals=0
        ),
        name="column_sums",
    )(meta, tiles)


def documents_kernel(docs, w_in, w_out_t, host, degrees, labels, out, total):
    step = pl.program_id(0)
    topics = w_out_t.shape[0]
    width = total.shape[1]

    hidden = jax.nn.gelu(
        jnp.dot(docs[...], w_in[...], preferred_element_type=jnp.float32), approximate=True
    ).astype(jnp.bfloat16)
    logits = lax.dot_general(w_out_t[...], hidden, NT, preferred_element_type=jnp.float32)
    powers = jnp.exp(logits - jnp.max(logits, axis=0, keepdims=True))
    probs = powers * (1.0 / jnp.sum(powers, axis=0, keepdims=True))
    high = probs.astype(jnp.bfloat16)
    low = (probs - high.astype(jnp.float32)).astype(jnp.bfloat16)
    index = host[0]
    digit = index // width
    within = index - digit * width
    picks = [jnp.where(digit == j, 1.0, 0.0).astype(jnp.bfloat16) for j in range(DIGITS)]
    left = jnp.concatenate([high * p for p in picks] + [low * p for p in picks], axis=0)
    places = lax.broadcasted_iota(jnp.int32, (width, index.shape[1]), 0)
    right = jnp.where(places == within, 1.0, 0.0).astype(jnp.bfloat16)
    added = lax.dot_general(left, right, NT, preferred_element_type=jnp.float32)

    @pl.when(step == 0)
    def _():
        total[...] = added

    @pl.when(step > 0)
    def _():
        total[...] += added

    @pl.when(step == pl.num_programs(0) - 1)
    def _():
        split, per, _ = out.shape
        hosts = DIGITS * width
        degree = sum(degrees[j] for j in range(1, degrees.shape[0])) + degrees[0]
        blocks, block = degree.shape
        for q in range(split):
            for d in range(DIGITS):
                first = d * topics + q * per
                second = first + DIGITS * topics
                out[q, :, d * width : (d + 1) * width] = (
                    total[first : first + per, :] + total[second : second + per, :]
                )
            for c in range(blocks // per):
                cols = slice(hosts + c * block, hosts + (c + 1) * block)
                out[q, :, cols] = degree[c * per : (c + 1) * per, :]
            wide = hosts + blocks // per * block
            out[q, :, wide:] = jnp.zeros((per, labels.shape[1]), jnp.float32)
            out[q, : labels.shape[0], wide:] = labels[...].astype(jnp.float32)


def document_topics(docs, w_in, w_out, doc_host, degrees, labels, hosts, split):
    count, depth = docs.shape
    hid, topics = w_out.shape
    per = topics // split
    width = hosts // DIGITS
    steps = count // DOC_BLOCK
    shape = (split, per, hosts + hosts // per + labels.shape[1])
    return pl.pallas_call(
        documents_kernel,
        grid=(steps,),
        in_specs=[
            pl.BlockSpec((DOC_BLOCK, depth), lambda i: (i, 0)),
            pl.BlockSpec((depth, hid), lambda i: (0, 0)),
            pl.BlockSpec((topics, hid), lambda i: (0, 0)),
            pl.BlockSpec((1, 1, DOC_BLOCK), lambda i: (i, 0, 0)),
            pl.BlockSpec(degrees.shape, lambda i: (0, 0, 0)),
            pl.BlockSpec(labels.shape, lambda i: (0, 0)),
        ],
        out_specs=pl.BlockSpec(shape, lambda i: (0, 0, 0)),
        scratch_shapes=[pltpu.VMEM((2 * DIGITS * topics, width), jnp.float32)],
        out_shape=jax.ShapeDtypeStruct(shape, jnp.float32),
        compiler_params=pltpu.CompilerParams(vmem_limit_bytes=56 * MIB),
        cost_estimate=pl.CostEstimate(
            flops=2 * count * (depth * hid + hid * topics + 2 * topics * hosts),
            bytes_accessed=docs.size * 2,
            transcendentals=count * (hid + topics),
        ),
        name="document_topics",
    )(docs, w_in, w_out.T, doc_host.reshape(steps, 1, DOC_BLOCK), degrees, labels)


def start_kernel(teleport, sums, late, sent, start, inverse, late_out):
    split, per, _ = sums.shape
    hosts = start.shape[1]
    blocks, block = teleport.shape
    member = teleport[...].astype(jnp.float32) * LIFT
    mass = jnp.zeros((per, 1), jnp.float32)
    tail = slice(hosts, hosts + inverse.shape[1])
    degree = sum(sums[j, :, tail] for j in range(1, split)) + sums[0, :, tail]
    inv = 1.0 / jnp.maximum(degree, 1.0)
    inverse[...] = inv
    for b in range(blocks):
        cols = slice(b * block, (b + 1) * block)
        value = sum(sums[j, :, cols] for j in range(1, split)) + sums[0, :, cols]
        value = value * member[b : b + 1, :]
        start[:, cols] = value
        c, r = b // per, b % per
        row = inv[r : r + 1, c * block : (c + 1) * block]
        scaled = (value * row).astype(jnp.bfloat16)
        for j in range(sent.shape[0]):
            sent[j, :, cols] = scaled
        mass = mass + jnp.sum(value, axis=1, keepdims=True)
    lane = lax.broadcasted_iota(jnp.int32, (per, block), 1)
    first = mass.astype(jnp.bfloat16).astype(jnp.float32)
    second = (mass - first).astype(jnp.bfloat16).astype(jnp.float32)
    third = mass - first - second
    pieces = jnp.where(
        lane == 0, first, jnp.where(lane == 1, second, jnp.where(lane == 2, third, 0.0))
    ).astype(jnp.bfloat16)
    for j in range(sent.shape[0]):
        sent[j, :, blocks * block :] = pieces


def start_values(teleport, sums, parts, block, late):
    _, per, _ = sums.shape
    hosts = teleport.shape[0]
    vmem = pl.BlockSpec(memory_space=pltpu.VMEM)
    keep = pl.BlockSpec(memory_space=pl.ANY)
    return pl.pallas_call(
        start_kernel,
        in_specs=[vmem, vmem, keep],
        out_specs=[vmem, vmem, vmem, keep],
        out_shape=[
            jax.ShapeDtypeStruct((parts, per, hosts + block), jnp.bfloat16),
            jax.ShapeDtypeStruct((per, hosts), jnp.float32),
            jax.ShapeDtypeStruct((per, hosts // per), jnp.float32),
            jax.ShapeDtypeStruct(late.shape, late.dtype),
        ],
        input_output_aliases={2: 3},
        compiler_params=pltpu.CompilerParams(vmem_limit_bytes=16 * MIB),
        name="start_values",
    )(teleport.reshape(hosts // block, block), sums, late)


def hop_kernel(first, last, split, scale, meta, place, shards, *rest):
    tiles, (tele, inverse), outs = rest[:split], rest[split : split + 2], rest[split + 2 : -2]
    slabs, inflow = rest[-2:]
    blocks, per, block = inflow.shape
    parts = shards.shape[0]
    slots = tiles[0].shape[0] * pl.num_programs(0)
    span = meta.shape[0] // split
    step = pl.program_id(0)

    @pl.when(step == 0)
    def _():
        inflow[...] = jnp.zeros_like(inflow)
        slabs[parts * blocks] = jnp.zeros(slabs.shape[1:], slabs.dtype)
        for j in range(parts):
            for b in range(blocks):
                slabs[j * blocks + b] = shards[j, :, b * block : (b + 1) * block]

    empty = jnp.zeros((per, block), jnp.bfloat16)
    for q in range(split):
        start = (place[0] ^ q) * span
        base = start + step * TILE_GROUP

        @pl.when(step * TILE_GROUP < meta[start + 2 * slots])
        def _():
            products = []
            for c in range(0, TILE_GROUP, 4):
                held = [slabs[meta[base + c + i]] for i in range(4)]
                left = jnp.concatenate(
                    [
                        jnp.concatenate([held[0], held[1], empty, empty], axis=0),
                        jnp.concatenate([empty, empty, held[2], held[3]], axis=0),
                    ],
                    axis=1,
                )
                right = jnp.concatenate(
                    [
                        tiles[q][c : c + 2].reshape(2 * block, block),
                        tiles[q][c + 2 : c + 4].reshape(2 * block, block),
                    ],
                    axis=1,
                )
                both = lax.dot_general(left, right, NT, preferred_element_type=jnp.float32)
                for i in range(4):
                    side = (i % 2) * block
                    products.append(both[i * per : (i + 1) * per, side : side + block])
            for i in range(TILE_GROUP):
                inflow[meta[base + slots + i]] += products[i]

    @pl.when(step == pl.num_programs(0) - 1)
    def _():
        if first:
            tail = sum(shards[j, :, blocks * block :].astype(jnp.float32) for j in range(parts))
            mass = jnp.sum(tail, axis=1, keepdims=True)
        for b in range(blocks):
            cols = slice(b * block, (b + 1) * block)
            own = tele[:, cols]
            state = 0.85 * inflow[b] + 0.15 * own
            if first:
                state = state / mass
                outs[1][:, cols] = own / mass
            if last:
                count = outs[0].shape[2] // block
                into = slice((b % count) * block, (b % count + 1) * block)
                outs[0][b // count, :, into] = state * scale
            else:
                c, r = b // per, b % per
                row = inverse[r : r + 1, c * block : (c + 1) * block]
                scaled = (state * row).astype(jnp.bfloat16)
                for j in range(parts):
                    outs[0][j, :, cols] = scaled


def hop(first, last, meta, place, shards, tiles, tele, inverse):
    per, hosts = tele.shape
    slots, block, _ = tiles[0].shape
    blocks = hosts // block
    parts, split = shards.shape[0], len(tiles)
    if last:
        out_shape = [jax.ShapeDtypeStruct((split, per, hosts // split), jnp.float32)]
    else:
        out_shape = [jax.ShapeDtypeStruct((parts, per, hosts), jnp.bfloat16)]
        if first:
            out_shape.append(jax.ShapeDtypeStruct((per, hosts), jnp.float32))

    def whole(array):
        return pl.BlockSpec(array.shape, lambda i, m, p: (0,) * len(array.shape))

    return pl.pallas_call(
        functools.partial(hop_kernel, first, last, split, float(parts * hosts)),
        grid_spec=pltpu.PrefetchScalarGridSpec(
            num_scalar_prefetch=2,
            grid=(slots // TILE_GROUP,),
            in_specs=[whole(shards)]
            + [pl.BlockSpec((TILE_GROUP, block, block), lambda i, m, p: (i, 0, 0))] * split
            + [whole(tele), whole(inverse)],
            out_specs=[whole(s) for s in out_shape],
            scratch_shapes=[
                pltpu.VMEM((parts * blocks + 1, per, block), jnp.bfloat16),
                pltpu.VMEM((blocks, per, block), jnp.float32),
            ],
        ),
        out_shape=out_shape,
        compiler_params=pltpu.CompilerParams(vmem_limit_bytes=32 * MIB),
        cost_estimate=pl.CostEstimate(
            flops=2 * split * slots * block * block * per,
            bytes_accessed=split * slots * block * block * 2,
            transcendentals=0,
        ),
        name="hop",
    )(meta, place, shards, *tiles, tele, inverse)


def swap(value, axis):
    return lax.all_to_all(value, axis, split_axis=0, concat_axis=0, tiled=True)


def body(docs, w_in, w_out, doc_host, tiles, dst_block, src_block, tile_count, teleport):
    hosts = teleport.shape[0]
    slots, block, _ = tiles.shape
    topics = w_out.shape[1]
    parts, split = lax.axis_size("hst"), lax.axis_size("doc")
    blocks = hosts // block

    used = jnp.arange(slots, dtype=jnp.int32) < tile_count[0]
    slab = jnp.where(used, src_block, parts * blocks)
    meta = jnp.concatenate([slab, dst_block, jnp.broadcast_to(tile_count, (2 * slots,))])
    labels = meta.reshape(-1, block)
    place = lax.axis_index("doc").astype(jnp.int32).reshape(1)

    sets = {0: tiles, 1: xor_send(tiles, "doc", 1)}
    for j in range(2, split, 2):
        sets[j] = xor_send(tiles, "doc", j)
    degrees = swap(column_sums(meta, tiles, parts, blocks), "hst")
    sums = swap(document_topics(docs, w_in, w_out, doc_host, degrees, labels, hosts, split), "doc")
    all_meta = sums[:, : labels.shape[0], -block:].astype(jnp.int32).reshape(-1)
    sent, tele, inverse, sets[2] = start_values(teleport, sums, parts, block, sets[2])
    for j in range(2, split, 2):
        sets[j + 1] = xor_send(sets[j], "doc", 1)
    all_tiles = [sets[j] for j in range(split)]
    for step in range(HOPS):
        first, last = step == 0, step == HOPS - 1
        outs = hop(first, last, all_meta, place, swap(sent, "hst"), all_tiles, tele, inverse)
        sent = outs[0]
        if first:
            tele = outs[1]
    return swap(sent, "doc").reshape(topics, hosts // split).T


def solution(mesh):
    placed = (
        P(("hst", "doc"), None),
        P(),
        P(),
        P(("hst", "doc")),
        P(("hst", "doc"), None, None),
        P(("hst", "doc")),
        P(("hst", "doc")),
        P(("hst", "doc")),
        P("hst"),
    )
    return jax.shard_map(
        body, mesh=mesh, in_specs=placed, out_specs=P(("hst", "doc"), None), check_vma=False
    )
```

time: 182 us -> 141 us (0.77)
  blocking collectives: 0 us -> 56.3 us
  waiting for transfers between devices: 80.7 us -> 29.8 us
  starting transfers between devices: 53.3 us -> 12.9 us
  local copies, waits for them, and re-layouts: 7.16 us -> 3.06 us
    ppermute x43 -> x3, waiting for transfers between devices: 80.7 us -> 0.01 us  [xor_send(): return lax.ppermute(value, axis, [(i, i ^ step) for i in range(size)])]
    all_to_all x0 -> x4, blocking collectives: none -> 56.3 us  [swap(): return lax.all_to_all(value, axis, split_axis=0, concat_axis=0, tiled=True)]
    ppermute x43 -> x3, starting transfers between devices: 53.3 us -> 3.43 us  [xor_send(): return lax.ppermute(value, axis, [(i, i ^ step) for i in range(size)])]
    all_to_all x0 -> x2, waiting for transfers between devices: none -> 29.8 us  [swap(): return lax.all_to_all(value, axis, split_axis=0, concat_axis=0, tiled=True)]
    all_to_all x0 -> x2, starting transfers between devices: none -> 9.51 us  [swap(): return lax.all_to_all(value, axis, split_axis=0, concat_axis=0, tiled=True)]
    unnamed x17 -> x9, local copies, waits for them, and re-layouts: 6.3 us -> 3.06 us
    pallas_call x6 -> x5, Pallas kernels: 36.4 us -> 35.3 us  [the longest x3 18.9 us: hop(): pl.pallas_call(functools.partial(hop_kernel, first, last, split, float(pa...]
  transfers between devices with their start and end apart: 43 -> 5, of which waited for: 23 -> 2; matrix products, arithmetic and copies ran while one was open for 1% -> 1% of each run, Pallas kernels for 8% -> 12%
where the time goes in v2:
time: 141 us
  blocking collectives  56.3 us (40%)
  Pallas kernels  36.4 us (26%)
  waiting for transfers between devices  29.8 us (21%)
  starting transfers between devices  12.9 us (9%)
  local copies, waits for them, and re-layouts  3.06 us (2%)
  other arithmetic  1.96 us (1%)
    all_to_all x4, blocking collectives, swap(): return lax.all_to_all(value, axis, split_axis=0, concat_axis=0, tiled=True)  56.3 us
    all_to_all x2, waiting for transfers between devices, swap(): return lax.all_to_all(value, axis, split_axis=0, concat_axis=0, tiled=True)  29.8 us
    pallas_call x3, Pallas kernels, hop(): pl.pallas_call(functools.partial(hop_kernel, first, last, split, float(pa...  18.9 us
    pallas_call x1, Pallas kernels, document_topics(): pl.pallas_call(documents_kernel, grid=(steps,), in_specs=[pl.BlockSpec((D...  16.3 us
    all_to_all x2, starting transfers between devices, swap(): return lax.all_to_all(value, axis, split_axis=0, concat_axis=0, tiled=True)  9.51 us
    ppermute x3, starting transfers between devices, xor_send(): return lax.ppermute(value, axis, [(i, i ^ step) for i in range(size)])  3.43 us
    unnamed x9, local copies, waits for them, and re-layouts  3.06 us
  transfers between devices with their start and end apart: 5, of which 2 were waited for; matrix products, arithmetic and copies ran while one was open for 1% of the time, Pallas kernels for 12%

profile of v2, /device:TPU:0, one launch (start us, length us, event | category | flops | bytes accessed | tf_op | source)
XLA Modules:
  0.0 141.3 jit_solution(9589999265577232911)
XLA Ops:
  0.0 3.0 %collective-permute-start = (bf16[64,128,128]{2,1,0:T(8,128)(2,1)}, bf16[64,128,128]{2,1,0:T(8,128)(2,1)}, u32[]{:S(2)}, u32[]{:S(2)}) collective-permute-start(bf16[64,128,128]{2,1,0:T(8,128)(2,1)} %rest_0_.5), channel_id=1, source_target_pairs={{0,2},{1,3},{2,0},{3,1},{4,6},{5,7},{6,4},{7,5},{8,10},{9,11},{10,... | collective-permute-start | bytes 6291464 | tf_op jit(solution)/shard_map/ppermute | solution.py:22
  3.6 0.7 compare_select_fusion
  4.3 1.3 fusion
  5.6 0.0 copy-start
  5.6 1.6 %copy-done = bf16[64,128,128]{2,1,0:T(8,128)(2,1)S(1)} copy-done((bf16[64,128,128]{2,1,0:T(8,128)(2,1)S(1)}, bf16[64,128,128]{2,1,0:T(8,128)(2,1)}, u32[]{:S(2)}) %copy-start) | copy-done | bytes 2097176
  7.2 1.1 column_sums.1
  8.3 12.6 %all_to_all.30.degrees = f32[8,16,128]{2,1,0:T(8,128)} all-to-all(f32[8,16,128]{2,1,0:T(8,128)S(1)} %column_sums.1), channel_id=1, replica_groups=mesh['hst'=8,'doc'=4] {'hst'}, dimensions={0} | all-to-all | bytes 131072 | tf_op jit(solution)/shard_map/all_to_all | solution.py:313
  20.9 0.0 copy-start.1
  20.9 0.0 copy-start.3
  20.9 16.3 %document_topics.1 = f32[4,16,2304]{2,1,0:T(8,128)} custom-call(bf16[8192,768]{1,0:T(8,128)(2,1)} %docs.1, bf16[768,256]{1,0:T(8,128)(2,1)} %w_in.1, bf16[64,256]{1,0:T(8,128)(2,1)} %bitcast.18, s32[8,1,1024]{2,1,0:T(1,128)} %bitcast.19, f32[8,16,128]{2,1,0:T(8,128)} %all_to_all.30.degrees, s32[2,128]{1,0:T(2,128)} %get-tuple-element.17.labels), custom_call_target="tpu_custom_call" | custom-call | flops 7784628224 | bytes 12582912 | tf_op jit(solution)/shard_map/document_topics/pallas_call | solution.py:123
  37.2 3.5 %all-to-all-start.1 = ((f32[4,16,2304]{2,1,0:T(8,128)}), f32[4,16,2304]{2,1,0:T(8,128)S(1)}, u32[]{:S(2)}, u32[]{:S(2)}) async-start(f32[4,16,2304]{2,1,0:T(8,128)} %document_topics.1), calls=%async_computation.1 | async-start | bytes 1179648 | tf_op jit(solution)/shard_map/all_to_all | solution.py:313
  40.7 0.0 copy-done.1
  40.7 0.5 collective-permute-start.1
  41.1 14.0 %all-to-all-done.1.sums = f32[4,16,2304]{2,1,0:T(8,128)S(1)} async-done(((f32[4,16,2304]{2,1,0:T(8,128)}), f32[4,16,2304]{2,1,0:T(8,128)S(1)}, u32[]{:S(2)}, u32[]{:S(2)}) %all-to-all-start.1) | async-done | bytes 589856 | tf_op jit(solution)/shard_map/all_to_all | solution.py:313
  55.1 0.0 collective-permute-done.late
  55.1 0.0 copy-done.3
  55.1 0.1 start_values.1
  55.3 0.0 copy-start.2
  55.3 0.8 copy-done.2
  56.1 0.0 collective-permute-start.2
  56.1 6.0 %all-to-all-start.2 = ((bf16[8,16,2176]{2,1,0:T(8,128)(2,1)}), bf16[8,16,2176]{2,1,0:T(8,128)(2,1)S(1)}, u32[]{:S(2)}, u32[]{:S(2)}) async-start(bf16[8,16,2176]{2,1,0:T(8,128)(2,1)} %copy-done.2), calls=%async_computation.2 | async-start | bytes 1114112 | tf_op jit(solution)/shard_map/all_to_all | solution.py:313
  62.1 0.0 collective-permute-done.1.rest_1_
  62.1 15.8 %all-to-all-done.2.shards = bf16[8,16,2176]{2,1,0:T(8,128)(2,1)S(1)} async-done(((bf16[8,16,2176]{2,1,0:T(8,128)(2,1)}), bf16[8,16,2176]{2,1,0:T(8,128)(2,1)S(1)}, u32[]{:S(2)}, u32[]{:S(2)}) %all-to-all-start.2) | async-done | bytes 557088 | tf_op jit(solution)/shard_map/all_to_all | solution.py:313
  78.0 0.0 collective-permute-done.2.rest_3_
  78.0 6.4 %hop.3 = (bf16[8,16,2048]{2,1,0:T(8,128)(2,1)S(1)}, f32[16,2048]{1,0:T(8,128)S(1)}) custom-call(s32[1024]{0:T(1024)S(1)} %bitcast.13, s32[1]{0:T(128)} %bitcast.5.place, bf16[8,16,2176]{2,1,0:T(8,128)(2,1)S(1)} %all-to-all-done.2.shards, bf16[64,128,128]{2,1,0:T(8,128)(2,1)S(1)} %copy-done.1, bf16[64,128,128]{2,1,0:T(8,128)(2,1)} %collective-permute-done.1.rest_1_, ...), custom_call_target="tpu_custom_call" | custom-call | flops 134217728 | bytes 8388608 | tf_op jit(solution)/shard_map/hop/pallas_call | solution.py:287
  84.4 18.5 %all_to_all.31.shards = bf16[8,16,2048]{2,1,0:T(8,128)(2,1)S(1)} all-to-all(bf16[8,16,2048]{2,1,0:T(8,128)(2,1)S(1)} %get-tuple-element.15), channel_id=1, replica_groups=mesh['hst'=8,'doc'=4] {'hst'}, dimensions={0} | all-to-all | bytes 1048576 | tf_op jit(solution)/shard_map/all_to_all | solution.py:313
  102.9 6.3 %hop.4 = bf16[8,16,2048]{2,1,0:T(8,128)(2,1)S(1)} custom-call(s32[1024]{0:T(1024)S(1)} %bitcast.14, s32[1]{0:T(128)} %bitcast.5.place, bf16[8,16,2048]{2,1,0:T(8,128)(2,1)S(1)} %all_to_all.31.shards, bf16[64,128,128]{2,1,0:T(8,128)(2,1)S(1)} %copy-done.1, bf16[64,128,128]{2,1,0:T(8,128)(2,1)} %collective-permute-done.1.rest_1_, ...), custom_call_target="tpu_custom_call" | custom-call | flops 134217728 | bytes 8388608 | tf_op jit(solution)/shard_map/hop/pallas_call | solution.py:287
  109.2 18.0 %all_to_all.32.shards = bf16[8,16,2048]{2,1,0:T(8,128)(2,1)S(1)} all-to-all(bf16[8,16,2048]{2,1,0:T(8,128)(2,1)S(1)} %hop.4), channel_id=1, replica_groups=mesh['hst'=8,'doc'=4] {'hst'}, dimensions={0} | all-to-all | bytes 1048576 | tf_op jit(solution)/shard_map/all_to_all | solution.py:313
  127.1 6.2 %hop.5 = f32[4,16,512]{2,1,0:T(8,128)S(1)} custom-call(s32[1024]{0:T(1024)S(1)} %bitcast.15, s32[1]{0:T(128)} %bitcast.5.place, bf16[8,16,2048]{2,1,0:T(8,128)(2,1)S(1)} %all_to_all.32.shards, bf16[64,128,128]{2,1,0:T(8,128)(2,1)S(1)} %copy-done.1, bf16[64,128,128]{2,1,0:T(8,128)(2,1)} %collective-permute-done.1.rest_1_, ...), custom_call_target="tpu_custom_call" | custom-call | flops 134217728 | bytes 8388608 | tf_op jit(solution)/shard_map/hop/pallas_call | solution.py:287
  133.3 7.3 %all_to_all.33 = f32[4,16,512]{2,1,0:T(8,128)S(1)} all-to-all(f32[4,16,512]{2,1,0:T(8,128)S(1)} %hop.5), channel_id=1, replica_groups=mesh['hst'=8,'doc'=4] {'doc'}, dimensions={0} | all-to-all | bytes 262144 | tf_op jit(solution)/shard_map/all_to_all | solution.py:313
  140.6 0.7 copy.14
  (2 shorter events, 0.0 us)
Async XLA Ops:
  0.0 55.1 %collective-permute-start = (bf16[64,128,128]{2,1,0:T(8,128)(2,1)}, bf16[64,128,128]{2,1,0:T(8,128)(2,1)}, u32[]{:S(2)}, u32[]{:S(2)}) collective-permute-start(bf16[64,128,128]{2,1,0:T(8,128)(2,1)} %rest_0_.5), channel_id=1, source_target_pairs={{0,2},{1,3},{2,0},{3,1},{4,6},{5,7},{6,4},{7,5},{8,10},{9,11},{10,... | collective-permute-start | bytes 6291464 | tf_op jit(solution)/shard_map/ppermute | solution.py:22
  5.6 1.6 %copy-start = (bf16[64,128,128]{2,1,0:T(8,128)(2,1)S(1)}, bf16[64,128,128]{2,1,0:T(8,128)(2,1)}, u32[]{:S(2)}) copy-start(bf16[64,128,128]{2,1,0:T(8,128)(2,1)} %rest_0_.5) | copy-start | bytes 6291460
  20.9 19.8 %copy-start.1 = (bf16[64,128,128]{2,1,0:T(8,128)(2,1)S(1)}, bf16[64,128,128]{2,1,0:T(8,128)(2,1)}, u32[]{:S(2)}) copy-start(bf16[64,128,128]{2,1,0:T(8,128)(2,1)} %rest_0_.5) | copy-start | bytes 6291460
  20.9 34.2 %copy-start.3 = (s32[2048]{0:T(1024)S(1)}, s32[2048]{0:T(1024)}, u32[]{:S(2)}) copy-start(s32[2048]{0:T(1024)} %param.17) | copy-start | bytes 24580
  37.2 17.9 %all-to-all-start.1 = ((f32[4,16,2304]{2,1,0:T(8,128)}), f32[4,16,2304]{2,1,0:T(8,128)S(1)}, u32[]{:S(2)}, u32[]{:S(2)}) async-start(f32[4,16,2304]{2,1,0:T(8,128)} %document_topics.1), calls=%async_computation.1 | async-start | bytes 1179648 | tf_op jit(solution)/shard_map/all_to_all | solution.py:313
  40.7 21.5 %collective-permute-start.1 = (bf16[64,128,128]{2,1,0:T(8,128)(2,1)S(1)}, bf16[64,128,128]{2,1,0:T(8,128)(2,1)}, u32[]{:S(2)}, u32[]{:S(2)}) collective-permute-start(bf16[64,128,128]{2,1,0:T(8,128)(2,1)S(1)} %copy-done.1), channel_id=1, source_target_pairs={{0,1},{1,0},{2,3},{3,2},{4,5},{5,4},{6,7},{7,6},{8,9},{9,8},{10,11... | collective-permute-start | bytes 6291464 | tf_op jit(solution)/shard_map/ppermute | solution.py:22
  55.3 0.8 copy-start.2
  56.1 21.9 %collective-permute-start.2 = (bf16[64,128,128]{2,1,0:T(8,128)(2,1)}, bf16[64,128,128]{2,1,0:T(8,128)(2,1)}, u32[]{:S(2)}, u32[]{:S(2)}) collective-permute-start(bf16[64,128,128]{2,1,0:T(8,128)(2,1)} %get-tuple-element.12.rest_2_), channel_id=1, source_target_pairs={{0,1},{1,0},{2,3},{3,2},{4,5},{5,4},{6,7},{7,6},{8,9},{9,8},{10,11... | collective-permute-start | bytes 6291464 | tf_op jit(solution)/shard_map/ppermute | solution.py:22
  56.1 21.9 %all-to-all-start.2 = ((bf16[8,16,2176]{2,1,0:T(8,128)(2,1)}), bf16[8,16,2176]{2,1,0:T(8,128)(2,1)S(1)}, u32[]{:S(2)}, u32[]{:S(2)}) async-start(bf16[8,16,2176]{2,1,0:T(8,128)(2,1)} %copy-done.2), calls=%async_computation.2 | async-start | bytes 1114112 | tf_op jit(solution)/shard_map/all_to_all | solution.py:313
